TPU v7x, 32 devices: a whole 2x2x4 slice. The times are simulated.
32 devices in a mesh: recon: 1, slab: 32 (over z, y, x, core), coil: 1.
Axes of the slice: x: 2, y: 2, z: 4, core: 2. Of those that a mesh axis runs over, the one named last changes fastest.
Arguments:
- image: float32 [2, 192, 192, 192], P('recon', 'slab'), may hold values from -6 to 6
- prox_point: float32 [2, 192, 192, 192], P('recon', 'slab'), may hold values from -6 to 6
- dual: float32 [2, 192, 192, 192], P('recon', 'slab'), may hold values from -6 to 6
- adjoint_data: float32 [2, 192, 192, 192], P('recon', 'slab'), may hold values from -6 to 6
- coil_maps: float32 [1, 2, 192, 192, 192], P('coil', 'recon', 'slab'), may hold values from -4 to 4
- kernel: float32 [384, 384, 384], P('slab'), may hold values from 0.05 to 5
Outputs:
- image_new: float32 [2, 192, 192, 192], P('recon', 'slab')
- prox_new: float32 [2, 192, 192, 192], P('recon', 'slab')
- dual_new: float32 [2, 192, 192, 192], P('recon', 'slab')
All inputs are finite; a program needn't handle non-finite values.
Results may differ from a plain program's by a relative error of at most 0.00015.
Values sent between devices are 32-bit elements; how exact they have to be, the bound alone decides.
No kernel may reach another device: no remote copies, remote signals or barrier semaphores. Data moves between devices by JAX's collectives and lax.ppermute only.
A program may use at most 192 MiB of HBM per device.

v0:
```python
import functools
import math

import jax
import jax.numpy as jnp
import ml_dtypes
import numpy as np
from jax import lax
from jax.experimental import pallas as pl
from jax.experimental.pallas import tpu as pltpu
from jax.sharding import PartitionSpec as P

half_root = 0.7071067811865476
shrink = 0.5
step_size = 0.25
penalty = 1.0
VMEM_LIMIT = 56 * 1024 * 1024


def real_form(rows, cols, length, direction, gain=1.0):
    angle = 2.0 * math.pi / length * (np.outer(rows, cols) % length).astype(np.float64)
    cosine = np.cos(angle) * gain
    sine = direction * np.sin(angle) * gain
    return np.concatenate(
        [np.concatenate([cosine, sine], 1), np.concatenate([-sine, cosine], 1)], 0
    )


def three_way(table, axis):
    high = table.astype(ml_dtypes.bfloat16)
    low = (table - high.astype(np.float64)).astype(ml_dtypes.bfloat16)
    return np.concatenate([high, high, low], axis)


def split(values):
    high = values.astype(jnp.bfloat16)
    low = (values - high.astype(jnp.float32)).astype(jnp.bfloat16)
    return high, low


def stacked(parts, axis):
    pairs = [split(part) for part in parts]
    highs = [pair[0] for pair in pairs]
    lows = [pair[1] for pair in pairs]
    return jnp.concatenate(highs + lows + highs, axis=axis)


def product(left, right):
    return jnp.dot(left, right, preferred_element_type=jnp.float32)


def coil_image(image_ref, coil_ref, right_ref):
    planes = image_ref.shape[1]
    reals, imags = [], []
    for plane in range(planes):
        img_r, img_i = image_ref[0, plane], image_ref[1, plane]
        map_r, map_i = coil_ref[0, plane], coil_ref[1, plane]
        reals.append(map_r * img_r - map_i * img_i)
        imags.append(map_r * img_i + map_i * img_r)
    right_ref[...] = stacked([jnp.concatenate(reals, axis=1), jnp.concatenate(imags, axis=1)], 0)


def lane_tiles(lanes):
    return [(tile, min(128, lanes - tile * 128)) for tile in range(pl.cdiv(lanes, 128))]


def put_rows(out_ref, count, lines, line, rows):
    pitch = out_ref.shape[0] // count
    for tile, size in lane_tiles(rows.shape[1]):
        cells = rows[:, tile * 128 : tile * 128 + size]
        if size < 128:
            cells = jnp.pad(cells, ((0, 0), (0, 128 - size)))
        out_ref[pl.ds(tile * lines + line, count, stride=pitch), :] = cells


def get_rows(data_ref, count, lines, line, tiles):
    pitch = data_ref.shape[0] // count
    return jnp.concatenate(
        [data_ref[pl.ds(tile * lines + line, count, stride=pitch), :] for tile in tiles], axis=1
    )


def spread(count, lines, right, table_ref, out_ref):
    cells = product(table_ref[...], right)
    for line in range(lines):
        put_rows(out_ref, count, lines, line, cells[line * count : (line + 1) * count])


def spread_first_kernel(count, lines, image_ref, coil_ref, table_ref, out_ref, right_ref):
    coil_image(image_ref, coil_ref, right_ref)
    spread(count, lines, right_ref[...], table_ref, out_ref)


def spread_kernel(count, lines, right_ref, table_ref, out_ref):
    spread(count, lines, right_ref[...], table_ref, out_ref)


def middle_kernel(count, planes, width, lines, data_ref, gain_ref, fx_ref, fz_ref, gz_ref, gx_ref, out_ref):
    step = pl.program_id(0)
    grid_len = gain_ref.shape[1]
    depth = count * planes
    tiles = range(pl.cdiv(planes * width, 128))

    def part_of(part):
        rows = get_rows(data_ref, count, lines, 2 * step + part, tiles)
        return jnp.concatenate(
            [rows[:, plane * width : (plane + 1) * width] for plane in range(planes)], axis=0
        )

    left = stacked([part_of(0), part_of(1)], 1)
    along_x = product(left, fx_ref[...])
    right = stacked([along_x[:, :grid_len], along_x[:, grid_len:]], 0)
    spectrum = product(fz_ref[...], right)
    gain = gain_ref[0]
    right = stacked([spectrum[:grid_len] * gain, spectrum[grid_len:] * gain], 0)
    along_x = product(gz_ref[...], right)
    left = stacked([along_x[:depth], along_x[depth:]], 1)
    cells = product(left, gx_ref[...])
    for part in range(2):
        rows = jnp.concatenate(
            [
                cells[plane * count : (plane + 1) * count, part * width : (part + 1) * width]
                for plane in range(planes)
            ],
            axis=1,
        )
        put_rows(out_ref, count, lines, 2 * step + part, rows)


def lines_back(count, lines, data_ref, table_ref, tiles):
    rows = [get_rows(data_ref, count, lines, line, tiles) for line in range(lines)]
    return product(table_ref[...], stacked([jnp.concatenate(rows, axis=0)], 0))


def back_kernel(count, lines, lanes, data_ref, table_ref, *refs):
    field = lines_back(count, lines, data_ref, table_ref, range(pl.cdiv(lanes, 128)))
    if len(refs) == 2:
        field = field + refs[0][...]
    refs[-1][...] = field


def plane_normal(field, coil_ref, plane, start):
    height, width = coil_ref.shape[-2:]
    real = field[:height, start : start + width]
    imag = field[height:, start : start + width]
    map_r, map_i = coil_ref[0, plane], coil_ref[1, plane]
    return map_r * real + map_i * imag, map_r * imag - map_i * real


def normal_kernel(field_ref, coil_ref, out_ref):
    planes, height, width = coil_ref.shape[1:]
    for plane in range(planes):
        out_ref[0, plane], out_ref[1, plane] = plane_normal(field_ref, coil_ref, plane, plane * width)


def edge_kernel(count, lines, data_ref, table_ref, part_ref, coil_ref, base_ref, dual_ref, low_ref, high_ref):
    planes, height, width = coil_ref.shape[1:]
    for plane, out_ref in ((0, low_ref), (planes - 1, high_ref)):
        first = plane * width // 128
        tiles = range(first, pl.cdiv((plane + 1) * width, 128))
        field = lines_back(count, lines, data_ref, table_ref, tiles)
        field = field + part_ref[:, tiles[0] * 128 : (tiles[-1] + 1) * 128]
        normal = plane_normal(field, coil_ref, plane, plane * width - first * 128)
        for part in range(2):
            image_new = base_ref[part, plane] - step_size * normal[part]
            out_ref[part] = image_new + dual_ref[part, plane]


THRESHOLD = shrink / (half_root**3)


def store_plane(ref, index, part, cells):
    height, width = cells.shape
    ref[index + (part, 0, slice(0, height))] = cells[:, :128]
    tail = jnp.concatenate([cells[:, 128:], cells[:, : 256 - width]], axis=1)
    ref[index + (part, 1, slice(0, height))] = tail
    ref[index + (part, 0, slice(height, height + 8))] = cells[:8, :128]
    ref[index + (part, 1, slice(height, height + 8))] = tail[:8]


def swap_pairs(values, even):
    return jnp.where(
        even, values + pltpu.roll(values, 127, 1), pltpu.roll(values, 1, 1) - values
    )


def spin_rows(offset, width, first, second):
    lane = lax.broadcasted_iota(jnp.int32, (8, 128), 1)
    even = lane % 2 == 0
    coefs = []
    for part in range(2):
        tiles = []
        for tile in range(2):
            a_0, a_1 = first(part, tile, 0), first(part, tile, 1)
            b_0, b_1 = second(part, tile, 0), second(part, tile, 1)
            sum_0, sum_1, dif_0, dif_1 = a_0 + b_0, a_1 + b_1, a_0 - b_0, a_1 - b_1
            tiles.append([sum_0 + sum_1, sum_0 - sum_1, dif_0 + dif_1, dif_0 - dif_1])
        if offset:
            for band in range(4):
                low, high = pltpu.roll(tiles[0][band], 127, 1), pltpu.roll(tiles[1][band], 127, 1)
                tiles[0][band] = jnp.where(lane == 127, high, low)
                tiles[1][band] = high
        coefs.append([[swap_pairs(band, even) for band in bands] for bands in tiles])
    for tile in range(2):
        for band in range(4):
            real, imag = coefs[0][tile][band], coefs[1][tile][band]
            square = jnp.maximum(real * real + imag * imag, THRESHOLD * THRESHOLD)
            factor = 1.0 - THRESHOLD * lax.rsqrt(square)
            if band == 0:
                factor = jnp.where(even, 1.0, factor)
            coefs[0][tile][band] = swap_pairs(real * factor, even)
            coefs[1][tile][band] = swap_pairs(imag * factor, even)
    scale = 0.5 * half_root**6
    spun = []
    for part in range(2):
        tiles = []
        for tile in range(2):
            bands = [band * scale for band in coefs[part][tile]]
            sum_0, sum_1 = bands[0] + bands[1], bands[0] - bands[1]
            dif_0, dif_1 = bands[2] + bands[3], bands[2] - bands[3]
            tiles.append([[sum_0 + dif_0, sum_1 + dif_1], [sum_0 - dif_0, sum_1 - dif_1]])
        if offset:
            for plane in range(2):
                for which in range(2):
                    low, high = tiles[0][plane][which], tiles[1][plane][which]
                    wrapped = pltpu.roll(high, 128 - (width - 129), 1)
                    tiles[1][plane][which] = jnp.where(
                        lane == 0, pltpu.roll(low, 1, 1), pltpu.roll(high, 1, 1)
                    )
                    tiles[0][plane][which] = jnp.where(lane == 0, wrapped, pltpu.roll(low, 1, 1))
        spun.append(tiles)
    return spun


def spin_pair(offset, height, width, load_first, load_second, store):
    def body(group, _):
        def rows_of(which):
            return pl.ds(group * 16 + offset + which, 8, stride=2)

        spun = spin_rows(
            offset,
            width,
            lambda part, tile, which: load_first(part, tile, rows_of(which)),
            lambda part, tile, which: load_second(part, tile, rows_of(which)),
        )
        for part in range(2):
            for tile in range(2):
                for plane in range(2):
                    for which in range(2):
                        store(plane, part, tile, rows_of(which), spun[part][tile][plane][which])
        return 0

    lax.fori_loop(0, height // 16, body, 0)


def finish_kernel(
    count, lines, data_ref, table_ref, part_ref, coil_ref, base_ref, dual_ref,
    image_ref, prox_ref, dual_out_ref, merged, total,
):
    planes, height, width = coil_ref.shape[1:]
    tiles = range(pl.cdiv(planes * width, 128))
    field = lines_back(count, lines, data_ref, table_ref, tiles) + part_ref[...]
    for plane in range(planes):
        normal = plane_normal(field, coil_ref, plane, plane * width)
        for part in range(2):
            image_new = base_ref[part, plane] - step_size * normal[part]
            image_ref[part, plane] = image_new
            store_plane(merged, (plane,), part, image_new + dual_ref[part, plane])

    def loader(plane):
        return lambda part, tile, rows: merged[plane, part, tile, rows, :]

    for low in range(0, planes, 2):

        def store(plane, part, tile, rows, cells, low=low):
            total[low + plane, part, tile, rows, :] = cells

        spin_pair(0, height, width, loader(low), loader(low + 1), store)
    total[:, :, :, height:, :] = jnp.zeros((planes, 2, 2, 8, 128), jnp.float32)
    for low in range(1, planes - 1, 2):

        def store(plane, part, tile, rows, cells, low=low):
            total[low + plane, part, tile, rows, :] += cells

        spin_pair(1, height, width, loader(low), loader(low + 1), store)
    for plane in range(planes):
        for part in range(2):
            for tile, size in ((0, 128), (1, width - 128)):
                lanes = slice(tile * 128, tile * 128 + size)
                total[plane, part, tile, :8, :] += total[plane, part, tile, height:, :]
                prox = total[plane, part, tile, :height, :size]
                prox_ref[part, plane, :, lanes] = prox
                dual_out_ref[part, plane, :, lanes] = merged[plane, part, tile, :height, :size] - prox


def rim_kernel(low_ref, high_ref, before_ref, after_ref, prox_ref, dual_ref, prox_out, dual_out, planes, total):
    height, width = low_ref.shape[-2:]
    is_low = pl.program_id(0) == 0
    for part in range(2):
        store_plane(planes, (0,), part, jnp.where(is_low, before_ref[part], high_ref[part]))
        store_plane(planes, (1,), part, jnp.where(is_low, low_ref[part], after_ref[part]))
    total[:, :, height:, :] = jnp.zeros((2, 2, 8, 128), jnp.float32)

    def loader(plane):
        return lambda part, tile, rows: planes[plane, part, tile, rows, :]

    kept = []

    def store(plane, part, tile, rows, cells):
        if plane == 0:
            kept.append(cells)
            return
        total[part, tile, rows, :] = jnp.where(is_low, cells, kept.pop(0))

    spin_pair(1, height, width, loader(0), loader(1), store)
    for part in range(2):
        for tile, size in ((0, 128), (1, width - 128)):
            lanes = slice(tile * 128, tile * 128 + size)
            total[part, tile, :1, :] = total[part, tile, height : height + 1, :]
            cells = total[part, tile, :height, :size]
            prox_out[part, 0, :, lanes] = prox_ref[part, 0, :, lanes] + cells
            dual_out[part, 0, :, lanes] = dual_ref[part, 0, :, lanes] - cells


def call(kernel, out_shape, micros, **extra):
    return pl.pallas_call(
        kernel,
        out_shape=out_shape,
        cost_estimate=pl.CostEstimate(
            flops=int(micros * 1e9), bytes_accessed=int(micros * 1e6), transcendentals=0
        ),
        compiler_params=pltpu.CompilerParams(vmem_limit_bytes=VMEM_LIMIT),
        **extra,
    )


def extended_2(cells, sides, width):
    for axis, dim in sides:
        count = lax.axis_size(axis)
        head = lax.slice_in_dim(cells, 0, width, axis=dim)
        tail = lax.slice_in_dim(cells, cells.shape[dim] - width, cells.shape[dim], axis=dim)
        cells = jnp.concatenate(
            [
                lax.ppermute(tail, axis, [(i, (i + 1) % count) for i in range(count)]),
                cells,
                lax.ppermute(head, axis, [((i + 1) % count, i) for i in range(count)]),
            ],
            axis=dim,
        )
    return cells


def pair_local(values, axis_dim, offset):
    length = values.shape[axis_dim]
    layout = [1] * values.ndim
    layout[axis_dim] = length
    is_first = ((jnp.arange(length) - offset) % 2 == 0).reshape(layout)
    after_one = jnp.roll(values, -1, axis_dim)
    before_one = jnp.roll(values, 1, axis_dim)
    return jnp.where(is_first, (values + after_one) * half_root, (before_one - values) * half_root)


def pair_planes(extended, own_first):
    middle = extended[:, 1:-1]
    after_one = extended[:, 2:]
    before_one = extended[:, :-2]
    marked = own_first[None, :, None, None]
    return jnp.where(marked, (middle + after_one) * half_root, (before_one - middle) * half_root)


def spin(extended, base, offset):
    total_planes = extended.shape[1]
    global_plane = base - 1 + jnp.arange(total_planes, dtype=jnp.int32)
    plane_first = (global_plane - offset) % 2 == 0
    own_first = plane_first[1:-1]
    lower_rim = (extended[:, :1] + extended[:, 1:2]) * half_root
    upper_rim = (extended[:, -2:-1] - extended[:, -1:]) * half_root
    coefs = jnp.concatenate([lower_rim, pair_planes(extended, own_first), upper_rim], axis=1)
    coefs = pair_local(coefs, 2, offset)
    coefs = pair_local(coefs, 3, offset)
    rows_first = (jnp.arange(extended.shape[2]) - offset) % 2 == 0
    cols_first = (jnp.arange(extended.shape[3]) - offset) % 2 == 0
    keep = plane_first[:, None, None] & rows_first[None, :, None] & cols_first[None, None, :]
    magnitude = jnp.sqrt(coefs[0] * coefs[0] + coefs[1] * coefs[1])
    factor = jnp.maximum(magnitude - shrink, 0.0) / jnp.maximum(magnitude, shrink)
    coefs = jnp.where(keep[None], coefs, coefs * factor[None])
    coefs = pair_local(coefs, 3, offset)
    coefs = pair_local(coefs, 2, offset)
    return pair_planes(coefs, own_first)


class Plan:
    def __init__(self, shape, lines, grid_len):
        self.count = count = lax.axis_size("slab")
        self.grid_len = grid_len
        _, self.planes, self.height, self.width = shape
        depth = count * self.planes
        self.chunks = chunks = 2 if lines % 2 == 0 else 1
        self.per_chunk = per_chunk = lines // chunks
        self.lines = per_chunk * 2
        self.lanes = self.planes * self.width
        self.padded = pl.cdiv(self.lanes, 128) * 128
        self.pitch = pl.cdiv(self.padded // 128 * self.lines, 8) * 8
        freq = np.arange(grid_len)

        def y_order(table, axis):
            order = np.arange(2 * grid_len).reshape(2, count, chunks, per_chunk)
            order = order.transpose(2, 3, 0, 1).reshape(chunks, -1)
            return [np.take(table, part, axis) for part in order]

        forward = real_form(np.arange(self.height), freq, grid_len, -1.0).T
        self.forward_y = [three_way(part, 1) for part in y_order(forward, 0)]
        back = real_form(freq, np.arange(self.height), grid_len, 1.0, 1.0 / grid_len).T
        self.back_y = [three_way(part, 1) for part in y_order(back, 1)]
        z_order = np.arange(depth).reshape(count, self.planes).T.reshape(depth)
        self.middle = (
            three_way(real_form(np.arange(self.width), freq, grid_len, -1.0), 0),
            three_way(real_form(z_order, freq, grid_len, -1.0).T, 1),
            three_way(real_form(freq, z_order, grid_len, 1.0, 1.0 / grid_len).T, 1),
            three_way(real_form(freq, np.arange(self.width), grid_len, 1.0, 1.0 / grid_len), 0),
        )


def returned_lines(plan, image, coil_map, gain_zx):
    count, lines = plan.count, plan.lines
    buffer = jax.ShapeDtypeStruct((count * plan.pitch, 128), jnp.float32)
    right = jax.ShapeDtypeStruct((6 * plan.height, plan.lanes), jnp.bfloat16)
    first, right = call(
        functools.partial(spread_first_kernel, count, lines), [buffer, right], 5
    )(image, coil_map, plan.forward_y[0])
    sent = [first]
    for chunk in range(1, plan.chunks):
        sent.append(
            call(functools.partial(spread_kernel, count, lines), buffer, 3)(
                right, plan.forward_y[chunk]
            )
        )

    def exchange(block):
        block = block.reshape(count, plan.pitch, 128)
        return lax.all_to_all(block, "slab", 0, 0, tiled=True).reshape(buffer.shape)

    whole = lambda array: pl.BlockSpec(array.shape, lambda step: (0,) * array.ndim)
    returned = []
    for chunk in range(plan.chunks):
        data = exchange(sent[chunk])
        at = functools.partial(lambda first, step: (first + step, 0, 0), chunk * plan.per_chunk)
        data = call(
            functools.partial(middle_kernel, count, plan.planes, plan.width, lines),
            buffer,
            5 * plan.per_chunk,
            grid=(plan.per_chunk,),
            in_specs=[whole(buffer), pl.BlockSpec((1,) + gain_zx.shape[1:], at)]
            + [whole(table) for table in plan.middle],
            out_specs=whole(buffer),
        )(data, gain_zx, *plan.middle)
        returned.append(exchange(data))
    return returned


def partial_field(plan, returned):
    field = jax.ShapeDtypeStruct((2 * plan.height, plan.padded), jnp.float32)
    total = ()
    for chunk, data in enumerate(returned):
        kernel = functools.partial(back_kernel, plan.count, plan.lines, plan.lanes)
        total = (call(kernel, field, 4)(data, plan.back_y[chunk], *total),)
    return total[0]


def neighbours(low, high):
    count = lax.axis_size("slab")
    before = lax.ppermute(high, "slab", [(i, (i + 1) % count) for i in range(count)])
    after = lax.ppermute(low, "slab", [((i + 1) % count, i) for i in range(count)])
    return before, after


def finish(plan, returned, coil_map, base, dual):
    planes, height, width = plan.planes, plan.height, plan.width
    part = partial_field(plan, returned[:-1])
    operands = (returned[-1], plan.back_y[-1], part, coil_map, base, dual)
    sizes = (plan.count, plan.lines)
    plane = jax.ShapeDtypeStruct((2, height, width), jnp.float32)
    low, high = call(functools.partial(edge_kernel, *sizes), [plane] * 2, 3)(*operands)
    before, after = neighbours(low, high)
    field = jax.ShapeDtypeStruct(dual.shape, jnp.float32)
    scratch = pltpu.VMEM((planes, 2, 2, height + 8, 128), jnp.float32)
    image_new, prox, dual_new = call(
        functools.partial(finish_kernel, *sizes), [field] * 3, 12, scratch_shapes=[scratch] * 2
    )(*operands)
    own = pl.BlockSpec((2, 1, height, width), lambda step: (0, step * (planes - 1), 0, 0))
    whole = pl.BlockSpec(plane.shape, lambda step: (0, 0, 0))
    prox, dual_new = call(
        rim_kernel,
        [field] * 2,
        3,
        grid=(2,),
        in_specs=[whole] * 4 + [own] * 2,
        out_specs=[own] * 2,
        input_output_aliases={4: 0, 5: 1},
        scratch_shapes=[
            pltpu.VMEM((2, 2, 2, height + 8, 128), jnp.float32),
            pltpu.VMEM((2, 2, height + 8, 128), jnp.float32),
        ],
    )(low, high, before, after, prox, dual_new)
    return image_new, prox, dual_new


def on_device(image, prox_point, dual, adjoint_data, coil_maps, kernel):
    plan = Plan(image.shape, *kernel.shape[:2])
    gain_zx = jnp.transpose(kernel, (0, 2, 1))
    base = image + step_size * (adjoint_data - penalty * (image - prox_point + dual))
    coils = coil_maps.shape[0]
    returned = [returned_lines(plan, image, coil_maps[coil], gain_zx) for coil in range(coils)]
    alone = coils * lax.axis_size("coil") == 1
    if alone and plan.planes % 2 == 0 and plan.height % 16 == 0 and 128 < plan.width < 256:
        return finish(plan, returned[0], coil_maps[0], base, dual)
    normal = jnp.zeros_like(image)
    for coil in range(coils):
        field = partial_field(plan, returned[coil])
        normal = normal + call(
            normal_kernel, jax.ShapeDtypeStruct(image.shape, jnp.float32), 3
        )(field, coil_maps[coil])
    normal = lax.psum(normal, "coil")
    image_new = base - step_size * normal
    merged = image_new + dual
    extended = extended_2(merged, (("slab", 1),), 1)
    first = lax.axis_index("slab") * plan.planes
    prox_new = 0.5 * (spin(extended, first, 0) + spin(extended, first, 1))
    return (image_new, prox_new, merged - prox_new)


def solution(mesh):
    in_specs = (
        P("recon", "slab", None, None),
        P("recon", "slab", None, None),
        P("recon", "slab", None, None),
        P("recon", "slab", None, None),
        P("coil", "recon", "slab", None, None),
        P("slab", None, None),
    )
    out_specs = (
        P("recon", "slab", None, None),
        P("recon", "slab", None, None),
        P("recon", "slab", None, None),
    )
    return jax.shard_map(
        on_device, mesh=mesh, in_specs=in_specs, out_specs=out_specs, check_vma=False
    )
```

profile of v0, /device:TPU:0, one launch (start us, length us, event | category | flops | bytes accessed | tf_op | source)
XLA Modules:
  0.0 250.6 jit_solution(12311996984508602726)
XLA Ops:
  0.6 5.7 %shard_map.157 = (f32[3584,128]{1,0:T(8,128)}, bf16[1152,1152]{1,0:T(8,128)(2,1)}) custom-call(f32[2,6,192,192]{3,2,1,0:T(8,128)} %image_ref.1, f32[2,6,192,192]{3,2,1,0:T(8,128)} %bitcast.12, bf16[384,1152]{1,0:T(8,128)(2,1)} %constant.18.clone.table_ref), custom_call_target="tpu_custom_call" | custom-call | flops 5000000000 | bytes 5000000 | tf_op jit(solution)/shard_map/pallas_call | solution.py:428
  6.3 7.3 %all-to-all-start.2 = ((f32[32,112,128]{2,1,0:T(8,128)}), f32[32,112,128]{2,1,0:T(8,128)S(1)}, u32[]{:S(2)}, u32[]{:S(2)}) async-start(f32[32,112,128]{2,1,0:T(8,128)} %bitcast.20), calls=%async_computation.2 | async-start | bytes 3670016 | tf_op jit(solution)/shard_map/all_to_all | solution.py:441
  13.6 4.8 %shard_map.158 = f32[3584,128]{1,0:T(8,128)} custom-call(bf16[1152,1152]{1,0:T(8,128)(2,1)} %get-tuple-element.12.right_ref, bf16[384,1152]{1,0:T(8,128)(2,1)} %constant.19.clone.table_ref), custom_call_target="tpu_custom_call" | custom-call | flops 3000000000 | bytes 3000000 | tf_op jit(solution)/shard_map/pallas_call | solution.py:434
  18.4 38.4 %all-to-all-done.2 = f32[32,112,128]{2,1,0:T(8,128)S(1)} async-done(((f32[32,112,128]{2,1,0:T(8,128)}), f32[32,112,128]{2,1,0:T(8,128)S(1)}, u32[]{:S(2)}, u32[]{:S(2)}) %all-to-all-start.2) | async-done | bytes 1835040 | tf_op jit(solution)/shard_map/all_to_all | solution.py:441
  56.8 0.0 copy-start.2
  56.8 1.2 copy-done.2
  58.1 4.0 %all-to-all-start = ((f32[32,112,128]{2,1,0:T(8,128)}), f32[32,112,128]{2,1,0:T(8,128)S(1)}, u32[]{:S(2)}, u32[]{:S(2)}) async-start(f32[32,112,128]{2,1,0:T(8,128)} %bitcast.19), calls=%async_computation | async-start | bytes 3670016 | tf_op jit(solution)/shard_map/all_to_all | solution.py:441
  62.1 8.1 %copy.19 = f32[12,384,384]{1,2,0:T(8,128)} copy(f32[12,384,384]{2,1,0:T(8,128)} %param.19) | data formatting | bytes 14155776 | tf_op args[5]
  70.2 26.6 %shard_map.160 = f32[3584,128]{1,0:T(8,128)} custom-call(f32[3584,128]{1,0:T(8,128)} %bitcast.16, f32[12,384,384]{2,1,0:T(8,128)} %bitcast.10, bf16[1152,768]{1,0:T(8,128)(2,1)} %constant.20.clone.fx_ref, bf16[768,1152]{1,0:T(8,128)(2,1)} %constant.21.clone.fz_ref, bf16[384,2304]{1,0:T(8,128)(2,1)} %constant.22.clone.gz_ref, ...), custom_call_target="tpu_custom_call" | custom-call | flops 30000001024 | bytes 30000000 | tf_op jit(solution)/shard_map/pallas_call | solution.py:448
  96.7 8.6 %all-to-all-done = f32[32,112,128]{2,1,0:T(8,128)S(1)} async-done(((f32[32,112,128]{2,1,0:T(8,128)}), f32[32,112,128]{2,1,0:T(8,128)S(1)}, u32[]{:S(2)}, u32[]{:S(2)}) %all-to-all-start) | async-done | bytes 1835040 | tf_op jit(solution)/shard_map/all_to_all | solution.py:441
  105.3 0.0 copy-start.1
  105.3 4.1 %all-to-all-start.3 = ((f32[32,112,128]{2,1,0:T(8,128)}), f32[32,112,128]{2,1,0:T(8,128)}, u32[]{:S(2)}, u32[]{:S(2)}) async-start(f32[32,112,128]{2,1,0:T(8,128)} %bitcast.18), calls=%async_computation.3 | async-start | bytes 3670016 | tf_op jit(solution)/shard_map/all_to_all | solution.py:441
  109.5 0.0 copy-done.1
  109.5 26.6 %shard_map.159 = f32[3584,128]{1,0:T(8,128)} custom-call(f32[3584,128]{1,0:T(8,128)} %bitcast.15, f32[12,384,384]{2,1,0:T(8,128)} %bitcast.11, bf16[1152,768]{1,0:T(8,128)(2,1)} %constant.20.clone.fx_ref, bf16[768,1152]{1,0:T(8,128)(2,1)} %constant.21.clone.fz_ref, bf16[384,2304]{1,0:T(8,128)(2,1)} %constant.22.clone.gz_ref, ...), custom_call_target="tpu_custom_call" | custom-call | flops 30000001024 | bytes 30000000 | tf_op jit(solution)/shard_map/pallas_call | solution.py:448
  136.1 0.0 copy-start
  136.1 16.6 %all-to-all-done.3 = f32[32,112,128]{2,1,0:T(8,128)} async-done(((f32[32,112,128]{2,1,0:T(8,128)}), f32[32,112,128]{2,1,0:T(8,128)}, u32[]{:S(2)}, u32[]{:S(2)}) %all-to-all-start.3) | async-done | bytes 1835040 | tf_op jit(solution)/shard_map/all_to_all | solution.py:441
  152.7 4.3 %all-to-all-start.1 = ((f32[32,112,128]{2,1,0:T(8,128)}), f32[32,112,128]{2,1,0:T(8,128)}, u32[]{:S(2)}, u32[]{:S(2)}) async-start(f32[32,112,128]{2,1,0:T(8,128)} %bitcast.17), calls=%async_computation.1 | async-start | bytes 3670016 | tf_op jit(solution)/shard_map/all_to_all | solution.py:441
  157.0 0.0 copy-done
  157.0 5.1 %multiply_add_fusion.base_ref = f32[2,6,192,192]{3,2,1,0:T(8,128)} fusion(f32[2,6,192,192]{3,2,1,0:T(8,128)} %image_ref.1, f32[2,6,192,192]{3,2,1,0:T(8,128)} %param.17, f32[2,6,192,192]{3,2,1,0:T(8,128)S(1)} %copy-done, f32[2,6,192,192]{3,2,1,0:T(8,128)} %param.15), kind=kLoop, calls=%fused_computation | loop fusion | flops 2211840 | bytes 8847360 | tf_op jit(solution)/shard_map/add | solution.py:511
  162.2 4.6 %shard_map.161.part_ref = f32[384,1152]{1,0:T(8,128)} custom-call(f32[3584,128]{1,0:T(8,128)} %bitcast.9.data_ref, bf16[384,1152]{1,0:T(8,128)(2,1)} %constant.24.clone.table_ref), custom_call_target="tpu_custom_call" | custom-call | flops 4000000000 | bytes 4000000 | tf_op jit(solution)/shard_map/pallas_call | solution.py:466
  166.8 33.4 %all-to-all-done.1 = f32[32,112,128]{2,1,0:T(8,128)} async-done(((f32[32,112,128]{2,1,0:T(8,128)}), f32[32,112,128]{2,1,0:T(8,128)}, u32[]{:S(2)}, u32[]{:S(2)}) %all-to-all-start.1) | async-done | bytes 1835040 | tf_op jit(solution)/shard_map/all_to_all | solution.py:441
  200.1 6.2 %shard_map.163 = (f32[2,192,192]{2,1,0:T(8,128)}, f32[2,192,192]{2,1,0:T(8,128)}) custom-call(f32[3584,128]{1,0:T(8,128)} %bitcast.5.data_ref, bf16[384,1152]{1,0:T(8,128)(2,1)} %constant.25.clone.table_ref, f32[384,1152]{1,0:T(8,128)} %shard_map.161.part_ref, f32[2,6,192,192]{3,2,1,0:T(8,128)} %bitcast.13, f32[2,6,192,192]{3,2,1,0:T(8,128)} %multiply_add_fusion.base_ref, ...), custom_call_target="tpu_custom_call" | custom-call | flops 3000000000 | bytes 3000000 | tf_op jit(solution)/shard_map/pallas_call | solution.py:483
  206.3 0.0 collective-permute-start
  206.3 5.3 %collective-permute-start.1 = (f32[2,192,192]{2,1,0:T(8,128)}, f32[2,192,192]{2,1,0:T(8,128)S(1)}, u32[]{:S(2)}, u32[]{:S(2)}) collective-permute-start(f32[2,192,192]{2,1,0:T(8,128)} %get-tuple-element.15.low_ref), channel_id=1, source_target_pairs={{1,0},{2,1},{3,2},{4,3},{5,4},{6,5},{7,6},{8,7},{9,8},{10,9},{11,1... | collective-permute-start | bytes 884744 | tf_op jit(solution)/shard_map/ppermute | solution.py:473
  211.6 26.3 %shard_map.162 = (f32[2,6,192,192]{3,2,1,0:T(8,128)}, f32[2,6,192,192]{3,2,1,0:T(8,128)}, f32[2,6,192,192]{3,2,1,0:T(8,128)}) custom-call(f32[3584,128]{1,0:T(8,128)} %bitcast.5.data_ref, bf16[384,1152]{1,0:T(8,128)(2,1)} %constant.25.clone.table_ref, f32[384,1152]{1,0:T(8,128)} %shard_map.161.part_ref, f32[2,6,192,192]{3,2,1,0:T(8,128)} %bitcast.14, ...), custom_call_target="tpu_custom_call" | custom-call | flops 12000000000 | bytes 12000000 | tf_op jit(solution)/shard_map/pallas_call | solution.py:487
  237.9 0.0 collective-permute-done.before_ref
  237.9 0.0 copy-start.3
  237.9 0.0 collective-permute-done.1.after_ref
  237.9 0.0 copy-start.4
  237.9 0.7 copy-done.3
  238.7 0.1 copy-done.4
  238.8 11.8 %shard_map.164 = (f32[2,6,192,192]{3,2,1,0:T(8,128)}, f32[2,6,192,192]{3,2,1,0:T(8,128)}) custom-call(f32[2,192,192]{2,1,0:T(8,128)} %get-tuple-element.15.low_ref, f32[2,192,192]{2,1,0:T(8,128)} %get-tuple-element.16.high_ref, f32[2,192,192]{2,1,0:T(8,128)} %copy-done.3, f32[2,192,192]{2,1,0:T(8,128)} %copy-done.4, ...), custom_call_target="tpu_custom_call", output_to_operand_aliasing={{0}: (4, {}), {1}: (5, {})} | custom-call | flops 3000000000 | bytes 3000000 | tf_op jit(solution)/shard_map/pallas_call | solution.py:492
Async XLA Ops:
  6.3 50.5 %all-to-all-start.2 = ((f32[32,112,128]{2,1,0:T(8,128)}), f32[32,112,128]{2,1,0:T(8,128)S(1)}, u32[]{:S(2)}, u32[]{:S(2)}) async-start(f32[32,112,128]{2,1,0:T(8,128)} %bitcast.20), calls=%async_computation.2 | async-start | bytes 3670016 | tf_op jit(solution)/shard_map/all_to_all | solution.py:441
  56.8 1.2 copy-start.2
  58.1 47.2 %all-to-all-start = ((f32[32,112,128]{2,1,0:T(8,128)}), f32[32,112,128]{2,1,0:T(8,128)S(1)}, u32[]{:S(2)}, u32[]{:S(2)}) async-start(f32[32,112,128]{2,1,0:T(8,128)} %bitcast.19), calls=%async_computation | async-start | bytes 3670016 | tf_op jit(solution)/shard_map/all_to_all | solution.py:441
  105.3 4.2 %copy-start.1 = (f32[32,112,128]{2,1,0:T(8,128)}, f32[32,112,128]{2,1,0:T(8,128)S(1)}, u32[]{:S(2)}) copy-start(f32[32,112,128]{2,1,0:T(8,128)S(1)} %all-to-all-done) | copy-start | bytes 5505028
  105.3 47.4 %all-to-all-start.3 = ((f32[32,112,128]{2,1,0:T(8,128)}), f32[32,112,128]{2,1,0:T(8,128)}, u32[]{:S(2)}, u32[]{:S(2)}) async-start(f32[32,112,128]{2,1,0:T(8,128)} %bitcast.18), calls=%async_computation.3 | async-start | bytes 3670016 | tf_op jit(solution)/shard_map/all_to_all | solution.py:441
  136.1 20.9 %copy-start = (f32[2,6,192,192]{3,2,1,0:T(8,128)S(1)}, f32[2,6,192,192]{3,2,1,0:T(8,128)}, u32[]{:S(2)}) copy-start(f32[2,6,192,192]{3,2,1,0:T(8,128)} %dual_ref.3) | copy-start | bytes 5308420
  152.7 47.5 %all-to-all-start.1 = ((f32[32,112,128]{2,1,0:T(8,128)}), f32[32,112,128]{2,1,0:T(8,128)}, u32[]{:S(2)}, u32[]{:S(2)}) async-start(f32[32,112,128]{2,1,0:T(8,128)} %bitcast.17), calls=%async_computation.1 | async-start | bytes 3670016 | tf_op jit(solution)/shard_map/all_to_all | solution.py:441
  206.3 31.6 %collective-permute-start = (f32[2,192,192]{2,1,0:T(8,128)}, f32[2,192,192]{2,1,0:T(8,128)S(1)}, u32[]{:S(2)}, u32[]{:S(2)}) collective-permute-start(f32[2,192,192]{2,1,0:T(8,128)} %get-tuple-element.16.high_ref), channel_id=1, source_target_pairs={{0,1},{1,2},{2,3},{3,4},{4,5},{5,6},{6,7},{7,8},{8,9},{9,10},{10,1... | collective-permute-start | bytes 884744 | tf_op jit(solution)/shard_map/ppermute | solution.py:472
  206.3 31.6 %collective-permute-start.1 = (f32[2,192,192]{2,1,0:T(8,128)}, f32[2,192,192]{2,1,0:T(8,128)S(1)}, u32[]{:S(2)}, u32[]{:S(2)}) collective-permute-start(f32[2,192,192]{2,1,0:T(8,128)} %get-tuple-element.15.low_ref), channel_id=1, source_target_pairs={{1,0},{2,1},{3,2},{4,3},{5,4},{6,5},{7,6},{8,7},{9,8},{10,9},{11,1... | collective-permute-start | bytes 884744 | tf_op jit(solution)/shard_map/ppermute | solution.py:473
  237.9 0.8 copy-start.3
  237.9 0.9 copy-start.4
where the time goes:
time: 251 us
  Pallas kernels  113 us (45%)
  waiting for transfers between devices  96.9 us (39%)
  starting transfers between devices  25.1 us (10%)
  local copies, waits for them, and re-layouts  10.2 us (4%)
  other arithmetic  5.15 us (2%)
    all_to_all x4, waiting for transfers between devices, exchange(): return lax.all_to_all(block, 'slab', 0, 0, tiled=True).reshape(buffer.shape)  96.9 us
    pallas_call x2, Pallas kernels, returned_lines(): call(functools.partial(middle_kernel, count, plan.planes, plan.width, lin...  53.1 us
    pallas_call x1, Pallas kernels, finish(): call(functools.partial(finish_kernel, *sizes), [field] * 3, 12, scratch_s...  26.3 us
    all_to_all x4, starting transfers between devices, exchange(): return lax.all_to_all(block, 'slab', 0, 0, tiled=True).reshape(buffer.shape)  19.8 us
    pallas_call x1, Pallas kernels, finish(): call(rim_kernel, [field] * 2, 3, grid=(2,), in_specs=[whole] * 4 + [own]...  11.8 us
    unnamed x11, local copies, waits for them, and re-layouts  10.2 us
    pallas_call x1, Pallas kernels, finish(): call(functools.partial(edge_kernel, *sizes), [plane] * 2, 3)(*operands)  6.17 us
    pallas_call x1, Pallas kernels, returned_lines(): call(functools.partial(spread_first_kernel, count, lines), [buffer, right...  5.69 us
  transfers between devices with their start and end apart: 6, of which 4 were waited for; matrix products, arithmetic and copies ran while one was open for 5% of the time, Pallas kernels for 35%

commit v1 on v0

--- a/solution.py
+++ b/solution.py
@@ -14,7 +14,7 @@
 shrink = 0.5
 step_size = 0.25
 penalty = 1.0
-VMEM_LIMIT = 56 * 1024 * 1024
+EPI = 28
 
 
 def real_form(rows, cols, length, direction, gain=1.0):
@@ -153,109 +153,9 @@
         out_ref[0, plane], out_ref[1, plane] = plane_normal(field_ref, coil_ref, plane, plane * width)
 
 
-def edge_kernel(count, lines, data_ref, table_ref, part_ref, coil_ref, base_ref, dual_ref, low_ref, high_ref):
-    planes, height, width = coil_ref.shape[1:]
-    for plane, out_ref in ((0, low_ref), (planes - 1, high_ref)):
-        first = plane * width // 128
-        tiles = range(first, pl.cdiv((plane + 1) * width, 128))
-        field = lines_back(count, lines, data_ref, table_ref, tiles)
-        field = field + part_ref[:, tiles[0] * 128 : (tiles[-1] + 1) * 128]
-        normal = plane_normal(field, coil_ref, plane, plane * width - first * 128)
-        for part in range(2):
-            image_new = base_ref[part, plane] - step_size * normal[part]
-            out_ref[part] = image_new + dual_ref[part, plane]
-
-
-THRESHOLD = shrink / (half_root**3)
-
-
-def store_plane(ref, index, part, cells):
-    height, width = cells.shape
-    ref[index + (part, 0, slice(0, height))] = cells[:, :128]
-    tail = jnp.concatenate([cells[:, 128:], cells[:, : 256 - width]], axis=1)
-    ref[index + (part, 1, slice(0, height))] = tail
-    ref[index + (part, 0, slice(height, height + 8))] = cells[:8, :128]
-    ref[index + (part, 1, slice(height, height + 8))] = tail[:8]
-
-
-def swap_pairs(values, even):
-    return jnp.where(
-        even, values + pltpu.roll(values, 127, 1), pltpu.roll(values, 1, 1) - values
-    )
-
-
-def spin_rows(offset, width, first, second):
-    lane = lax.broadcasted_iota(jnp.int32, (8, 128), 1)
-    even = lane % 2 == 0
-    coefs = []
-    for part in range(2):
-        tiles = []
-        for tile in range(2):
-            a_0, a_1 = first(part, tile, 0), first(part, tile, 1)
-            b_0, b_1 = second(part, tile, 0), second(part, tile, 1)
-            sum_0, sum_1, dif_0, dif_1 = a_0 + b_0, a_1 + b_1, a_0 - b_0, a_1 - b_1
-            tiles.append([sum_0 + sum_1, sum_0 - sum_1, dif_0 + dif_1, dif_0 - dif_1])
-        if offset:
-            for band in range(4):
-                low, high = pltpu.roll(tiles[0][band], 127, 1), pltpu.roll(tiles[1][band], 127, 1)
-                tiles[0][band] = jnp.where(lane == 127, high, low)
-                tiles[1][band] = high
-        coefs.append([[swap_pairs(band, even) for band in bands] for bands in tiles])
-    for tile in range(2):
-        for band in range(4):
-            real, imag = coefs[0][tile][band], coefs[1][tile][band]
-            square = jnp.maximum(real * real + imag * imag, THRESHOLD * THRESHOLD)
-            factor = 1.0 - THRESHOLD * lax.rsqrt(square)
-            if band == 0:
-                factor = jnp.where(even, 1.0, factor)
-            coefs[0][tile][band] = swap_pairs(real * factor, even)
-            coefs[1][tile][band] = swap_pairs(imag * factor, even)
-    scale = 0.5 * half_root**6
-    spun = []
-    for part in range(2):
-        tiles = []
-        for tile in range(2):
-            bands = [band * scale for band in coefs[part][tile]]
-            sum_0, sum_1 = bands[0] + bands[1], bands[0] - bands[1]
-            dif_0, dif_1 = bands[2] + bands[3], bands[2] - bands[3]
-            tiles.append([[sum_0 + dif_0, sum_1 + dif_1], [sum_0 - dif_0, sum_1 - dif_1]])
-        if offset:
-            for plane in range(2):
-                for which in range(2):
-                    low, high = tiles[0][plane][which], tiles[1][plane][which]
-                    wrapped = pltpu.roll(high, 128 - (width - 129), 1)
-                    tiles[1][plane][which] = jnp.where(
-                        lane == 0, pltpu.roll(low, 1, 1), pltpu.roll(high, 1, 1)
-                    )
-                    tiles[0][plane][which] = jnp.where(lane == 0, wrapped, pltpu.roll(low, 1, 1))
-        spun.append(tiles)
-    return spun
-
-
-def spin_pair(offset, height, width, load_first, load_second, store):
-    def body(group, _):
-        def rows_of(which):
-            return pl.ds(group * 16 + offset + which, 8, stride=2)
-
-        spun = spin_rows(
-            offset,
-            width,
-            lambda part, tile, which: load_first(part, tile, rows_of(which)),
-            lambda part, tile, which: load_second(part, tile, rows_of(which)),
-        )
-        for part in range(2):
-            for tile in range(2):
-                for plane in range(2):
-                    for which in range(2):
-                        store(plane, part, tile, rows_of(which), spun[part][tile][plane][which])
-        return 0
-
-    lax.fori_loop(0, height // 16, body, 0)
-
-
-def finish_kernel(
+def update_kernel(
     count, lines, data_ref, table_ref, part_ref, coil_ref, base_ref, dual_ref,
-    image_ref, prox_ref, dual_out_ref, merged, total,
+    image_ref, merged_ref, low_ref, high_ref,
 ):
     planes, height, width = coil_ref.shape[1:]
     tiles = range(pl.cdiv(planes * width, 128))
@@ -264,72 +164,131 @@
         normal = plane_normal(field, coil_ref, plane, plane * width)
         for part in range(2):
             image_new = base_ref[part, plane] - step_size * normal[part]
+            merged = image_new + dual_ref[part, plane]
             image_ref[part, plane] = image_new
-            store_plane(merged, (plane,), part, image_new + dual_ref[part, plane])
-
-    def loader(plane):
-        return lambda part, tile, rows: merged[plane, part, tile, rows, :]
-
+            merged_ref[part, plane] = merged
+            if plane == 0:
+                low_ref[part] = merged
+            if plane == planes - 1:
+                high_ref[part] = merged
+
+
+THRESHOLD = shrink / (half_root**3)
+
+
+def pairing(width, offset):
+    table = np.zeros((width, 256))
+    for pair in range(width // 2):
+        first, second = (2 * pair + offset) % width, (2 * pair + 1 + offset) % width
+        table[first, pair] = table[second, pair] = table[first, 128 + pair] = 1.0
+        table[second, 128 + pair] = -1.0
+    return table
+
+
+def pairing_tables(width, offset):
+    table = pairing(width, offset)
+    padded = np.concatenate([table, np.zeros((256 - width, 256))], 0)
+    to_pairs = np.concatenate([padded, padded], 0).astype(ml_dtypes.bfloat16)
+    back = np.concatenate([table.T, table.T], 0).astype(ml_dtypes.bfloat16)
+    return to_pairs, back
+
+
+def pair_lanes(cells, table_ref, band_ref, index):
+    height, width = cells.shape
+    high, low = split(jnp.pad(cells, ((0, 0), (0, 256 - width))))
+    bands = product(jnp.concatenate([high, low], axis=1), table_ref[...])
+    for tile in range(2):
+        band = bands[:, tile * 128 : tile * 128 + 128]
+        band_ref[index + (tile, slice(0, height))] = band
+        band_ref[index + (tile, slice(height, height + 8))] = band[:8]
+
+
+def unpair_lanes(table_ref, band_ref, index, height):
+    parts = [split(band_ref[index + (tile, slice(0, height))]) for tile in range(2)]
+    left = [part[0] for part in parts] + [part[1] for part in parts]
+    return product(jnp.concatenate(left, axis=1), table_ref[...])
+
+
+def shrink_planes(offset, height, band_ref, first, second):
+    scale = 0.5 * half_root**6
+    refs = (first, second)
+
+    def body(group, _):
+        picks = [pl.ds(group * 16 + offset + which, 8, stride=2) for which in range(2)]
+        for tile in range(2):
+            coefs = []
+            for part in range(2):
+                (a_0, a_1), (b_0, b_1) = (
+                    [band_ref[plane, part, tile, pick, :] for pick in picks] for plane in refs
+                )
+                sum_0, sum_1, dif_0, dif_1 = a_0 + b_0, a_1 + b_1, a_0 - b_0, a_1 - b_1
+                coefs.append([sum_0 + sum_1, sum_0 - sum_1, dif_0 + dif_1, dif_0 - dif_1])
+            for band in range(4):
+                real, imag = coefs[0][band], coefs[1][band]
+                if band == 0 and tile == 0:
+                    factor = scale
+                else:
+                    square = jnp.maximum(real * real + imag * imag, THRESHOLD * THRESHOLD)
+                    factor = scale - (scale * THRESHOLD) * lax.rsqrt(square)
+                coefs[0][band], coefs[1][band] = real * factor, imag * factor
+            for part in range(2):
+                bands = coefs[part]
+                sum_0, sum_1 = bands[0] + bands[1], bands[0] - bands[1]
+                dif_0, dif_1 = bands[2] + bands[3], bands[2] - bands[3]
+                spun = ((sum_0 + dif_0, sum_1 + dif_1), (sum_0 - dif_0, sum_1 - dif_1))
+                for plane, rows in zip(refs, spun):
+                    for pick, row in zip(picks, rows):
+                        band_ref[plane, part, tile, pick, :] = row
+        return 0
+
+    lax.fori_loop(0, height // 16, body, 0, unroll=2)
+
+
+def spin_0_kernel(merged_ref, to_ref, back_ref, out_ref, bands):
+    _, planes, height, _ = merged_ref.shape
     for low in range(0, planes, 2):
-
-        def store(plane, part, tile, rows, cells, low=low):
-            total[low + plane, part, tile, rows, :] = cells
-
-        spin_pair(0, height, width, loader(low), loader(low + 1), store)
-    total[:, :, :, height:, :] = jnp.zeros((planes, 2, 2, 8, 128), jnp.float32)
-    for low in range(1, planes - 1, 2):
-
-        def store(plane, part, tile, rows, cells, low=low):
-            total[low + plane, part, tile, rows, :] += cells
-
-        spin_pair(1, height, width, loader(low), loader(low + 1), store)
-    for plane in range(planes):
-        for part in range(2):
-            for tile, size in ((0, 128), (1, width - 128)):
-                lanes = slice(tile * 128, tile * 128 + size)
-                total[plane, part, tile, :8, :] += total[plane, part, tile, height:, :]
-                prox = total[plane, part, tile, :height, :size]
-                prox_ref[part, plane, :, lanes] = prox
-                dual_out_ref[part, plane, :, lanes] = merged[plane, part, tile, :height, :size] - prox
-
-
-def rim_kernel(low_ref, high_ref, before_ref, after_ref, prox_ref, dual_ref, prox_out, dual_out, planes, total):
-    height, width = low_ref.shape[-2:]
-    is_low = pl.program_id(0) == 0
-    for part in range(2):
-        store_plane(planes, (0,), part, jnp.where(is_low, before_ref[part], high_ref[part]))
-        store_plane(planes, (1,), part, jnp.where(is_low, low_ref[part], after_ref[part]))
-    total[:, :, height:, :] = jnp.zeros((2, 2, 8, 128), jnp.float32)
-
-    def loader(plane):
-        return lambda part, tile, rows: planes[plane, part, tile, rows, :]
-
-    kept = []
-
-    def store(plane, part, tile, rows, cells):
-        if plane == 0:
-            kept.append(cells)
-            return
-        total[part, tile, rows, :] = jnp.where(is_low, cells, kept.pop(0))
-
-    spin_pair(1, height, width, loader(0), loader(1), store)
-    for part in range(2):
-        for tile, size in ((0, 128), (1, width - 128)):
-            lanes = slice(tile * 128, tile * 128 + size)
-            total[part, tile, :1, :] = total[part, tile, height : height + 1, :]
-            cells = total[part, tile, :height, :size]
-            prox_out[part, 0, :, lanes] = prox_ref[part, 0, :, lanes] + cells
-            dual_out[part, 0, :, lanes] = dual_ref[part, 0, :, lanes] - cells
-
-
-def call(kernel, out_shape, micros, **extra):
+        for plane in (low, low + 1):
+            for part in range(2):
+                pair_lanes(merged_ref[part, plane], to_ref, bands, (plane, part))
+        shrink_planes(0, height, bands, low, low + 1)
+        for plane in (low, low + 1):
+            for part in range(2):
+                out_ref[part, plane] = unpair_lanes(back_ref, bands, (plane, part), height)
+
+
+def spin_1_kernel(merged_ref, before_ref, after_ref, half_ref, to_ref, back_ref, prox_ref, dual_ref, bands):
+    _, planes, height, _ = merged_ref.shape
+
+    def cells_of(plane, part):
+        if plane < 0:
+            return before_ref[part]
+        return after_ref[part] if plane == planes else merged_ref[part, plane]
+
+    for low in range(-1, planes, 2):
+        for plane in (low, low + 1):
+            for part in range(2):
+                pair_lanes(cells_of(plane, part), to_ref, bands, (plane + 1, part))
+        shrink_planes(1, height, bands, low + 1, low + 2)
+        for plane in (low, low + 1):
+            if 0 <= plane < planes:
+                for part in range(2):
+                    for tile in range(2):
+                        at = (plane + 1, part, tile)
+                        bands[at + (slice(0, 1),)] = bands[at + (slice(height, height + 1),)]
+                    spun = unpair_lanes(back_ref, bands, (plane + 1, part), height)
+                    prox = half_ref[part, plane] + spun
+                    prox_ref[part, plane] = prox
+                    dual_ref[part, plane] = merged_ref[part, plane] - prox
+
+
+def call(kernel, out_shape, micros, vmem=56, **extra):
     return pl.pallas_call(
         kernel,
         out_shape=out_shape,
         cost_estimate=pl.CostEstimate(
             flops=int(micros * 1e9), bytes_accessed=int(micros * 1e6), transcendentals=0
         ),
-        compiler_params=pltpu.CompilerParams(vmem_limit_bytes=VMEM_LIMIT),
+        compiler_params=pltpu.CompilerParams(vmem_limit_bytes=vmem * 1024 * 1024),
         **extra,
     )
 
@@ -477,31 +436,19 @@
 def finish(plan, returned, coil_map, base, dual):
     planes, height, width = plan.planes, plan.height, plan.width
     part = partial_field(plan, returned[:-1])
-    operands = (returned[-1], plan.back_y[-1], part, coil_map, base, dual)
-    sizes = (plan.count, plan.lines)
     plane = jax.ShapeDtypeStruct((2, height, width), jnp.float32)
-    low, high = call(functools.partial(edge_kernel, *sizes), [plane] * 2, 3)(*operands)
+    field = jax.ShapeDtypeStruct(dual.shape, jnp.float32)
+    image_new, merged, low, high = call(
+        functools.partial(update_kernel, plan.count, plan.lines), [field] * 2 + [plane] * 2, 8, EPI
+    )(returned[-1], plan.back_y[-1], part, coil_map, base, dual)
     before, after = neighbours(low, high)
-    field = jax.ShapeDtypeStruct(dual.shape, jnp.float32)
-    scratch = pltpu.VMEM((planes, 2, 2, height + 8, 128), jnp.float32)
-    image_new, prox, dual_new = call(
-        functools.partial(finish_kernel, *sizes), [field] * 3, 12, scratch_shapes=[scratch] * 2
-    )(*operands)
-    own = pl.BlockSpec((2, 1, height, width), lambda step: (0, step * (planes - 1), 0, 0))
-    whole = pl.BlockSpec(plane.shape, lambda step: (0, 0, 0))
-    prox, dual_new = call(
-        rim_kernel,
-        [field] * 2,
-        3,
-        grid=(2,),
-        in_specs=[whole] * 4 + [own] * 2,
-        out_specs=[own] * 2,
-        input_output_aliases={4: 0, 5: 1},
-        scratch_shapes=[
-            pltpu.VMEM((2, 2, 2, height + 8, 128), jnp.float32),
-            pltpu.VMEM((2, 2, height + 8, 128), jnp.float32),
-        ],
-    )(low, high, before, after, prox, dual_new)
+    bands = lambda held: [pltpu.VMEM((held, 2, 2, height + 8, 128), jnp.float32)]
+    half = call(spin_0_kernel, field, 5, EPI, scratch_shapes=bands(planes))(
+        merged, *pairing_tables(width, 0)
+    )
+    prox, dual_new = call(spin_1_kernel, [field] * 2, 6, EPI, scratch_shapes=bands(planes + 2))(
+        merged, before, after, half, *pairing_tables(width, 1)
+    )
     return image_new, prox, dual_new
 
 

time: 251 us -> 228 us (0.908)
  Pallas kernels: 113 us -> 81.8 us
  local copies, waits for them, and re-layouts: 10.2 us -> 14.1 us
  waiting for transfers between devices: 96.9 us -> 99.8 us
    pallas_call x3, Pallas kernels: 44.3 us -> 13.5 us  [the longest x1 5.7 us: finish(): call(spin_1_kernel, [field] * 2, 6, EPI, scratch_shapes=bands(planes + 2))]
    unnamed x11 -> x23, local copies, waits for them, and re-layouts: 10.2 us -> 14.1 us
    ppermute x1, waiting for transfers between devices: 0.01 us -> 2.84 us  [neighbours(): lax.ppermute(high, 'slab', [(i, (i + 1) % count) for i in range(count)])]
  transfers between devices with their start and end apart: 6 -> 6, of which waited for: 4 -> 5; matrix products, arithmetic and copies ran while one was open for 5% -> 6% of each run, Pallas kernels for 35% -> 29%
where the time goes in v1:
time: 228 us; the launch traced here: 227 us
  waiting for transfers between devices  99.8 us (44%)
  Pallas kernels  81.8 us (36%)
  starting transfers between devices  25.1 us (11%)
  local copies, waits for them, and re-layouts  14.1 us (6%)
  other arithmetic  5.12 us (2%)
    all_to_all x4, waiting for transfers between devices, exchange(): return lax.all_to_all(block, 'slab', 0, 0, tiled=True).reshape(buffer.shape)  96.9 us
    pallas_call x2, Pallas kernels, returned_lines(): call(functools.partial(middle_kernel, count, plan.planes, plan.width, lin...  53.1 us
    all_to_all x4, starting transfers between devices, exchange(): return lax.all_to_all(block, 'slab', 0, 0, tiled=True).reshape(buffer.shape)  19.8 us
    unnamed x23, local copies, waits for them, and re-layouts  14.1 us
    pallas_call x1, Pallas kernels, finish(): call(spin_1_kernel, [field] * 2, 6, EPI, scratch_shapes=bands(planes + 2))  5.7 us
    pallas_call x1, Pallas kernels, returned_lines(): call(functools.partial(spread_first_kernel, count, lines), [buffer, right...  5.69 us
    ppermute x1, starting transfers between devices, neighbours(): lax.ppermute(low, 'slab', [((i + 1) % count, i) for i in range(count)])  5.34 us
    add x1, other arithmetic, on_device(): image + step_size * (adjoint_data - penalty * (image - prox_point + dual))  5.12 us
  transfers between devices with their start and end apart: 6, of which 5 were waited for; matrix products, arithmetic and copies ran while one was open for 6% of the time, Pallas kernels for 29%

profile of v1, /device:TPU:0, one launch (start us, length us, event | category | flops | bytes accessed | tf_op | source)
XLA Modules:
  0.0 226.6 jit_solution(10352212204638314516)
XLA Ops:
  0.6 5.7 %shard_map.193 = (f32[3584,128]{1,0:T(8,128)}, bf16[1152,1152]{1,0:T(8,128)(2,1)}) custom-call(f32[2,6,192,192]{3,2,1,0:T(8,128)} %image_ref.1, f32[2,6,192,192]{3,2,1,0:T(8,128)} %bitcast.10, bf16[384,1152]{1,0:T(8,128)(2,1)} %constant.26.clone.table_ref), custom_call_target="tpu_custom_call" | custom-call | flops 5000000000 | bytes 5000000 | tf_op jit(solution)/shard_map/pallas_call | solution.py:387
  6.3 7.3 %all-to-all-start.2 = ((f32[32,112,128]{2,1,0:T(8,128)}), f32[32,112,128]{2,1,0:T(8,128)S(1)}, u32[]{:S(2)}, u32[]{:S(2)}) async-start(f32[32,112,128]{2,1,0:T(8,128)} %bitcast.19), calls=%async_computation.2 | async-start | bytes 3670016 | tf_op jit(solution)/shard_map/all_to_all | solution.py:400
  13.6 4.8 %shard_map.194 = f32[3584,128]{1,0:T(8,128)} custom-call(bf16[1152,1152]{1,0:T(8,128)(2,1)} %get-tuple-element.11.right_ref, bf16[384,1152]{1,0:T(8,128)(2,1)} %constant.27.clone.table_ref), custom_call_target="tpu_custom_call" | custom-call | flops 3000000000 | bytes 3000000 | tf_op jit(solution)/shard_map/pallas_call | solution.py:393
  18.4 38.4 %all-to-all-done.2 = f32[32,112,128]{2,1,0:T(8,128)S(1)} async-done(((f32[32,112,128]{2,1,0:T(8,128)}), f32[32,112,128]{2,1,0:T(8,128)S(1)}, u32[]{:S(2)}, u32[]{:S(2)}) %all-to-all-start.2) | async-done | bytes 1835040 | tf_op jit(solution)/shard_map/all_to_all | solution.py:400
  56.8 0.0 copy-start.10
  56.8 1.2 copy-done.10
  58.1 4.0 %all-to-all-start = ((f32[32,112,128]{2,1,0:T(8,128)}), f32[32,112,128]{2,1,0:T(8,128)S(1)}, u32[]{:S(2)}, u32[]{:S(2)}) async-start(f32[32,112,128]{2,1,0:T(8,128)} %bitcast.18), calls=%async_computation | async-start | bytes 3670016 | tf_op jit(solution)/shard_map/all_to_all | solution.py:400
  62.1 8.1 %copy.21 = f32[12,384,384]{1,2,0:T(8,128)} copy(f32[12,384,384]{2,1,0:T(8,128)} %param.23) | data formatting | bytes 14155776 | tf_op args[5]
  70.2 26.6 %shard_map.196 = f32[3584,128]{1,0:T(8,128)} custom-call(f32[3584,128]{1,0:T(8,128)} %bitcast.15, f32[12,384,384]{2,1,0:T(8,128)} %bitcast.12, bf16[1152,768]{1,0:T(8,128)(2,1)} %constant.28.clone.fx_ref, bf16[768,1152]{1,0:T(8,128)(2,1)} %constant.29.clone.fz_ref, bf16[384,2304]{1,0:T(8,128)(2,1)} %constant.30.clone.gz_ref, ...), custom_call_target="tpu_custom_call" | custom-call | flops 30000001024 | bytes 30000000 | tf_op jit(solution)/shard_map/pallas_call | solution.py:407
  96.7 8.6 %all-to-all-done = f32[32,112,128]{2,1,0:T(8,128)S(1)} async-done(((f32[32,112,128]{2,1,0:T(8,128)}), f32[32,112,128]{2,1,0:T(8,128)S(1)}, u32[]{:S(2)}, u32[]{:S(2)}) %all-to-all-start) | async-done | bytes 1835040 | tf_op jit(solution)/shard_map/all_to_all | solution.py:400
  105.3 0.0 copy-start.9
  105.3 4.1 %all-to-all-start.3 = ((f32[32,112,128]{2,1,0:T(8,128)}), f32[32,112,128]{2,1,0:T(8,128)}, u32[]{:S(2)}, u32[]{:S(2)}) async-start(f32[32,112,128]{2,1,0:T(8,128)} %bitcast.17), calls=%async_computation.3 | async-start | bytes 3670016 | tf_op jit(solution)/shard_map/all_to_all | solution.py:400
  109.5 0.0 copy-done.9
  109.5 26.6 %shard_map.195 = f32[3584,128]{1,0:T(8,128)} custom-call(f32[3584,128]{1,0:T(8,128)} %bitcast.14, f32[12,384,384]{2,1,0:T(8,128)} %bitcast.13, bf16[1152,768]{1,0:T(8,128)(2,1)} %constant.28.clone.fx_ref, bf16[768,1152]{1,0:T(8,128)(2,1)} %constant.29.clone.fz_ref, bf16[384,2304]{1,0:T(8,128)(2,1)} %constant.30.clone.gz_ref, ...), custom_call_target="tpu_custom_call" | custom-call | flops 30000001024 | bytes 30000000 | tf_op jit(solution)/shard_map/pallas_call | solution.py:407
  136.1 0.0 copy-start
  136.1 16.6 %all-to-all-done.3 = f32[32,112,128]{2,1,0:T(8,128)} async-done(((f32[32,112,128]{2,1,0:T(8,128)}), f32[32,112,128]{2,1,0:T(8,128)}, u32[]{:S(2)}, u32[]{:S(2)}) %all-to-all-start.3) | async-done | bytes 1835040 | tf_op jit(solution)/shard_map/all_to_all | solution.py:400
  152.7 4.3 %all-to-all-start.1 = ((f32[32,112,128]{2,1,0:T(8,128)}), f32[32,112,128]{2,1,0:T(8,128)}, u32[]{:S(2)}, u32[]{:S(2)}) async-start(f32[32,112,128]{2,1,0:T(8,128)} %bitcast.16), calls=%async_computation.1 | async-start | bytes 3670016 | tf_op jit(solution)/shard_map/all_to_all | solution.py:400
  157.0 0.0 copy-done
  157.0 5.1 %multiply_add_fusion.base_ref = f32[2,6,192,192]{3,2,1,0:T(8,128)} fusion(f32[2,6,192,192]{3,2,1,0:T(8,128)} %image_ref.1, f32[2,6,192,192]{3,2,1,0:T(8,128)} %param.21, f32[2,6,192,192]{3,2,1,0:T(8,128)S(1)} %copy-done, f32[2,6,192,192]{3,2,1,0:T(8,128)} %param.19), kind=kLoop, calls=%fused_computation | loop fusion | flops 2211840 | bytes 8847360 | tf_op jit(solution)/shard_map/add | solution.py:458
  162.1 0.0 copy-start.3
  162.1 4.7 %shard_map.197.part_ref = f32[384,1152]{1,0:T(8,128)} custom-call(f32[3584,128]{1,0:T(8,128)} %bitcast.9.data_ref, bf16[384,1152]{1,0:T(8,128)(2,1)} %constant.32.clone.table_ref), custom_call_target="tpu_custom_call" | custom-call | flops 4000000000 | bytes 4000000 | tf_op jit(solution)/shard_map/pallas_call | solution.py:425
  166.8 33.3 %all-to-all-done.1 = f32[32,112,128]{2,1,0:T(8,128)} async-done(((f32[32,112,128]{2,1,0:T(8,128)}), f32[32,112,128]{2,1,0:T(8,128)}, u32[]{:S(2)}, u32[]{:S(2)}) %all-to-all-start.1) | async-done | bytes 1835040 | tf_op jit(solution)/shard_map/all_to_all | solution.py:400
  200.1 0.0 copy-done.3
  200.1 0.0 copy-start.1
  200.1 1.7 copy-done.1
  201.8 0.0 copy-start.2
  201.8 1.7 copy-done.2
  203.4 0.0 copy-start.8
  203.5 1.5 copy-done.8
  204.9 0.0 copy-start.6
  204.9 0.0 copy-start.7
  204.9 5.0 %shard_map.198 = (f32[2,6,192,192]{3,2,1,0:T(8,128)}, f32[2,6,192,192]{3,2,1,0:T(8,128)S(1)}, f32[2,192,192]{2,1,0:T(8,128)S(1)}, f32[2,192,192]{2,1,0:T(8,128)S(1)}) custom-call(f32[3584,128]{1,0:T(8,128)} %bitcast.5.data_ref, bf16[384,1152]{1,0:T(8,128)(2,1)S(1)} %copy-done.3, f32[384,1152]{1,0:T(8,128)S(1)} %copy-done.8, f32[2,6,192,192]{3,2,1,0:T(8,128)S(1)} %bitcast.11, ...), custom_call_target="tpu_custom_call" | custom-call | flops 8000000000 | bytes 8000000 | tf_op jit(solution)/shard_map/pallas_call | solution.py:441
  210.0 0.0 collective-permute-start
  210.0 5.3 %collective-permute-start.1 = (f32[2,192,192]{2,1,0:T(8,128)S(1)}, f32[2,192,192]{2,1,0:T(8,128)S(1)}, u32[]{:S(2)}, u32[]{:S(2)}) collective-permute-start(f32[2,192,192]{2,1,0:T(8,128)S(1)} %get-tuple-element.16), channel_id=1, source_target_pairs={{1,0},{2,1},{3,2},{4,3},{5,4},{6,5},{7,6},{8,7},{9,8},{10,9},{11,1... | collective-permute-start | bytes 884744 | tf_op jit(solution)/shard_map/ppermute | solution.py:432
  215.3 0.0 copy-done.6
  215.3 0.0 copy-done.7
  215.3 0.0 copy-start.4
  215.3 0.0 copy-start.5
  215.3 2.7 %shard_map.199.half_ref = f32[2,6,192,192]{3,2,1,0:T(8,128)S(1)} custom-call(f32[2,6,192,192]{3,2,1,0:T(8,128)S(1)} %get-tuple-element.14.merged_ref, bf16[512,256]{1,0:T(8,128)(2,1)S(1)} %copy-done.6, bf16[512,192]{1,0:T(8,128)(2,1)S(1)} %copy-done.7), custom_call_target="tpu_custom_call" | custom-call | flops 5000000000 | bytes 5000000 | tf_op jit(solution)/shard_map/pallas_call | solution.py:446
  218.0 2.8 %collective-permute-done.before_ref = f32[2,192,192]{2,1,0:T(8,128)S(1)} collective-permute-done((f32[2,192,192]{2,1,0:T(8,128)S(1)}, f32[2,192,192]{2,1,0:T(8,128)S(1)}, u32[]{:S(2)}, u32[]{:S(2)}) %collective-permute-start) | collective-permute-done | bytes 294944 | tf_op jit(solution)/shard_map/ppermute | solution.py:431
  220.9 0.0 collective-permute-done.1.after_ref
  220.9 0.0 copy-done.4
  220.9 0.0 copy-done.5
  220.9 5.7 %shard_map.200 = (f32[2,6,192,192]{3,2,1,0:T(8,128)}, f32[2,6,192,192]{3,2,1,0:T(8,128)}) custom-call(f32[2,6,192,192]{3,2,1,0:T(8,128)S(1)} %get-tuple-element.14.merged_ref, f32[2,192,192]{2,1,0:T(8,128)S(1)} %collective-permute-done.before_ref, f32[2,192,192]{2,1,0:T(8,128)S(1)} %collective-permute-done.1.after_ref, ...), custom_call_target="tpu_custom_call" | custom-call | flops 6000000000 | bytes 6000000 | tf_op jit(solution)/shard_map/pallas_call | solution.py:449
Async XLA Ops:
  6.3 50.5 %all-to-all-start.2 = ((f32[32,112,128]{2,1,0:T(8,128)}), f32[32,112,128]{2,1,0:T(8,128)S(1)}, u32[]{:S(2)}, u32[]{:S(2)}) async-start(f32[32,112,128]{2,1,0:T(8,128)} %bitcast.19), calls=%async_computation.2 | async-start | bytes 3670016 | tf_op jit(solution)/shard_map/all_to_all | solution.py:400
  56.8 1.2 copy-start.10
  58.1 47.2 %all-to-all-start = ((f32[32,112,128]{2,1,0:T(8,128)}), f32[32,112,128]{2,1,0:T(8,128)S(1)}, u32[]{:S(2)}, u32[]{:S(2)}) async-start(f32[32,112,128]{2,1,0:T(8,128)} %bitcast.18), calls=%async_computation | async-start | bytes 3670016 | tf_op jit(solution)/shard_map/all_to_all | solution.py:400
  105.3 4.2 %copy-start.9 = (f32[32,112,128]{2,1,0:T(8,128)}, f32[32,112,128]{2,1,0:T(8,128)S(1)}, u32[]{:S(2)}) copy-start(f32[32,112,128]{2,1,0:T(8,128)S(1)} %all-to-all-done) | copy-start | bytes 5505028
  105.3 47.4 %all-to-all-start.3 = ((f32[32,112,128]{2,1,0:T(8,128)}), f32[32,112,128]{2,1,0:T(8,128)}, u32[]{:S(2)}, u32[]{:S(2)}) async-start(f32[32,112,128]{2,1,0:T(8,128)} %bitcast.17), calls=%async_computation.3 | async-start | bytes 3670016 | tf_op jit(solution)/shard_map/all_to_all | solution.py:400
  136.1 20.9 %copy-start = (f32[2,6,192,192]{3,2,1,0:T(8,128)S(1)}, f32[2,6,192,192]{3,2,1,0:T(8,128)}, u32[]{:S(2)}) copy-start(f32[2,6,192,192]{3,2,1,0:T(8,128)} %dual_ref.1) | copy-start | bytes 5308420
  152.7 47.5 %all-to-all-start.1 = ((f32[32,112,128]{2,1,0:T(8,128)}), f32[32,112,128]{2,1,0:T(8,128)}, u32[]{:S(2)}, u32[]{:S(2)}) async-start(f32[32,112,128]{2,1,0:T(8,128)} %bitcast.16), calls=%async_computation.1 | async-start | bytes 3670016 | tf_op jit(solution)/shard_map/all_to_all | solution.py:400
  162.1 38.0 %copy-start.3 = (bf16[384,1152]{1,0:T(8,128)(2,1)S(1)}, bf16[384,1152]{1,0:T(8,128)(2,1)}, u32[]{:S(2)}) copy-start(bf16[384,1152]{1,0:T(8,128)(2,1)} %constant.33.clone.table_ref) | copy-start | bytes 2654212
  200.1 1.7 copy-start.1
  201.8 1.7 copy-start.2
  203.4 1.5 copy-start.8
  204.9 10.4 %copy-start.6 = (bf16[512,256]{1,0:T(8,128)(2,1)S(1)}, bf16[512,256]{1,0:T(8,128)(2,1)}, u32[]{:S(2)}) copy-start(bf16[512,256]{1,0:T(8,128)(2,1)} %constant.34.clone.to_ref) | copy-start | bytes 786436
  204.9 10.4 %copy-start.7 = (bf16[512,192]{1,0:T(8,128)(2,1)S(1)}, bf16[512,192]{1,0:T(8,128)(2,1)}, u32[]{:S(2)}) copy-start(bf16[512,192]{1,0:T(8,128)(2,1)} %constant.35.clone.back_ref) | copy-start | bytes 589828
  210.0 10.9 %collective-permute-start = (f32[2,192,192]{2,1,0:T(8,128)S(1)}, f32[2,192,192]{2,1,0:T(8,128)S(1)}, u32[]{:S(2)}, u32[]{:S(2)}) collective-permute-start(f32[2,192,192]{2,1,0:T(8,128)S(1)} %get-tuple-element.15), channel_id=1, source_target_pairs={{0,1},{1,2},{2,3},{3,4},{4,5},{5,6},{6,7},{7,8},{8,9},{9,10},{10,1... | collective-permute-start | bytes 884744 | tf_op jit(solution)/shard_map/ppermute | solution.py:431
  210.0 10.9 %collective-permute-start.1 = (f32[2,192,192]{2,1,0:T(8,128)S(1)}, f32[2,192,192]{2,1,0:T(8,128)S(1)}, u32[]{:S(2)}, u32[]{:S(2)}) collective-permute-start(f32[2,192,192]{2,1,0:T(8,128)S(1)} %get-tuple-element.16), channel_id=1, source_target_pairs={{1,0},{2,1},{3,2},{4,3},{5,4},{6,5},{7,6},{8,7},{9,8},{10,9},{11,1... | collective-permute-start | bytes 884744 | tf_op jit(solution)/shard_map/ppermute | solution.py:432
  215.3 5.6 %copy-start.4 = (bf16[512,256]{1,0:T(8,128)(2,1)S(1)}, bf16[512,256]{1,0:T(8,128)(2,1)}, u32[]{:S(2)}) copy-start(bf16[512,256]{1,0:T(8,128)(2,1)} %constant.36.clone.to_ref) | copy-start | bytes 786436
  215.3 5.6 %copy-start.5 = (bf16[512,192]{1,0:T(8,128)(2,1)S(1)}, bf16[512,192]{1,0:T(8,128)(2,1)}, u32[]{:S(2)}) copy-start(bf16[512,192]{1,0:T(8,128)(2,1)} %constant.37.clone.back_ref) | copy-start | bytes 589828

commit v2 on v1

--- a/solution.py
+++ b/solution.py
@@ -14,7 +14,7 @@
 shrink = 0.5
 step_size = 0.25
 penalty = 1.0
-EPI = 28
+SMALL = 28
 
 
 def real_form(rows, cols, length, direction, gain=1.0):
@@ -49,28 +49,17 @@
     return jnp.dot(left, right, preferred_element_type=jnp.float32)
 
 
-def coil_image(image_ref, coil_ref, right_ref):
-    planes = image_ref.shape[1]
-    reals, imags = [], []
-    for plane in range(planes):
-        img_r, img_i = image_ref[0, plane], image_ref[1, plane]
-        map_r, map_i = coil_ref[0, plane], coil_ref[1, plane]
-        reals.append(map_r * img_r - map_i * img_i)
-        imags.append(map_r * img_i + map_i * img_r)
-    right_ref[...] = stacked([jnp.concatenate(reals, axis=1), jnp.concatenate(imags, axis=1)], 0)
-
-
 def lane_tiles(lanes):
     return [(tile, min(128, lanes - tile * 128)) for tile in range(pl.cdiv(lanes, 128))]
 
 
-def put_rows(out_ref, count, lines, line, rows):
+def put_rows(out_ref, count, lines, line, rows, skipped=0):
     pitch = out_ref.shape[0] // count
     for tile, size in lane_tiles(rows.shape[1]):
         cells = rows[:, tile * 128 : tile * 128 + size]
         if size < 128:
             cells = jnp.pad(cells, ((0, 0), (0, 128 - size)))
-        out_ref[pl.ds(tile * lines + line, count, stride=pitch), :] = cells
+        out_ref[pl.ds((skipped + tile) * lines + line, count, stride=pitch), :] = cells
 
 
 def get_rows(data_ref, count, lines, line, tiles):
@@ -80,51 +69,75 @@
     )
 
 
-def spread(count, lines, right, table_ref, out_ref):
-    cells = product(table_ref[...], right)
-    for line in range(lines):
-        put_rows(out_ref, count, lines, line, cells[line * count : (line + 1) * count])
-
-
-def spread_first_kernel(count, lines, image_ref, coil_ref, table_ref, out_ref, right_ref):
-    coil_image(image_ref, coil_ref, right_ref)
-    spread(count, lines, right_ref[...], table_ref, out_ref)
-
-
-def spread_kernel(count, lines, right_ref, table_ref, out_ref):
-    spread(count, lines, right_ref[...], table_ref, out_ref)
+def spread_kernel(count, lines, image_ref, coil_ref, table_ref, out_ref, image, coil, table, arrived):
+    planes, _, _, width = image.shape
+    copies = [pltpu.make_async_copy(table_ref, table, arrived.at[2 * planes])]
+    for plane in range(planes):
+        copies.append(
+            pltpu.make_async_copy(image_ref.at[:, plane], image.at[plane], arrived.at[2 * plane])
+        )
+        copies.append(
+            pltpu.make_async_copy(coil_ref.at[:, plane], coil.at[plane], arrived.at[2 * plane + 1])
+        )
+    for copy in copies[1:3] + copies[:1] + copies[3:]:
+        copy.start()
+    for low in range(0, planes, 2):
+        reals, imags = [], []
+        for plane in range(low, min(low + 2, planes)):
+            copies[1 + 2 * plane].wait()
+            copies[2 + 2 * plane].wait()
+            img_r, img_i, map_r, map_i = image[plane, 0], image[plane, 1], coil[plane, 0], coil[plane, 1]
+            reals.append(map_r * img_r - map_i * img_i)
+            imags.append(map_r * img_i + map_i * img_r)
+        right = stacked([jnp.concatenate(reals, axis=1), jnp.concatenate(imags, axis=1)], 0)
+        if low == 0:
+            copies[0].wait()
+        cells = product(table[...], right)
+        for line in range(lines):
+            rows = cells[line * count : (line + 1) * count]
+            put_rows(out_ref, count, lines, line, rows, low * width // 128)
 
 
 def middle_kernel(count, planes, width, lines, data_ref, gain_ref, fx_ref, fz_ref, gz_ref, gx_ref, out_ref):
-    step = pl.program_id(0)
-    grid_len = gain_ref.shape[1]
+    group, grid_len, _ = gain_ref.shape
+    first = 2 * group * pl.program_id(0)
     depth = count * planes
     tiles = range(pl.cdiv(planes * width, 128))
-
-    def part_of(part):
-        rows = get_rows(data_ref, count, lines, 2 * step + part, tiles)
-        return jnp.concatenate(
-            [rows[:, plane * width : (plane + 1) * width] for plane in range(planes)], axis=0
+    each = range(group)
+
+    def cells_of(one, part):
+        rows = get_rows(data_ref, count, lines, first + 2 * one + part, tiles)
+        return [rows[:, plane * width : (plane + 1) * width] for plane in range(planes)]
+
+    def side_by_side(cells):
+        return jnp.concatenate(cells, axis=1)
+
+    left = [jnp.concatenate(sum([cells_of(one, part) for one in each], []), axis=0) for part in range(2)]
+    along_x = product(stacked(left, 1), fx_ref[...])
+    right = [
+        side_by_side(
+            [along_x[one * depth : (one + 1) * depth, part * grid_len : (part + 1) * grid_len] for one in each]
         )
-
-    left = stacked([part_of(0), part_of(1)], 1)
-    along_x = product(left, fx_ref[...])
-    right = stacked([along_x[:, :grid_len], along_x[:, grid_len:]], 0)
-    spectrum = product(fz_ref[...], right)
-    gain = gain_ref[0]
+        for part in range(2)
+    ]
+    spectrum = product(fz_ref[...], stacked(right, 0))
+    gain = side_by_side([gain_ref[one].T for one in each])
     right = stacked([spectrum[:grid_len] * gain, spectrum[grid_len:] * gain], 0)
     along_x = product(gz_ref[...], right)
-    left = stacked([along_x[:depth], along_x[depth:]], 1)
-    cells = product(left, gx_ref[...])
-    for part in range(2):
-        rows = jnp.concatenate(
-            [
-                cells[plane * count : (plane + 1) * count, part * width : (part + 1) * width]
-                for plane in range(planes)
-            ],
-            axis=1,
+    left = [
+        jnp.concatenate(
+            [along_x[part * depth : (part + 1) * depth, one * grid_len : (one + 1) * grid_len] for one in each],
+            axis=0,
         )
-        put_rows(out_ref, count, lines, 2 * step + part, rows)
+        for part in range(2)
+    ]
+    cells = product(stacked(left, 1), gx_ref[...])
+    for one in each:
+        for part in range(2):
+            start = [one * depth + plane * count for plane in range(planes)]
+            lanes = slice(part * width, (part + 1) * width)
+            rows = side_by_side([cells[at : at + count, lanes] for at in start])
+            put_rows(out_ref, count, lines, first + 2 * one + part, rows)
 
 
 def lines_back(count, lines, data_ref, table_ref, tiles):
@@ -153,24 +166,55 @@
         out_ref[0, plane], out_ref[1, plane] = plane_normal(field_ref, coil_ref, plane, plane * width)
 
 
+def packed(ref):
+    halves = []
+    for part in range(2):
+        halves.append(jnp.concatenate([ref[part, plane] for plane in range(ref.shape[1])], axis=1))
+    return jnp.concatenate(halves, axis=0)
+
+
+def conj_product(coil, field):
+    half = coil.shape[0] // 2
+    map_r, map_i, real, imag = coil[:half], coil[half:], field[:half], field[half:]
+    return jnp.concatenate([map_r * real + map_i * imag, map_r * imag - map_i * real], axis=0)
+
+
+def prepare_kernel(
+    count, lines, data_ref, table_ref, image_ref, prox_ref, dual_ref, adjoint_ref, coil_ref, out_ref
+):
+    _, planes, _, width = coil_ref.shape
+    field = lines_back(count, lines, data_ref, table_ref, range(planes * width // 128))
+    image, coil, dual = packed(image_ref), packed(coil_ref), packed(dual_ref)
+    rest = penalty * (image - packed(prox_ref) + dual) - packed(adjoint_ref)
+    out_ref[0] = image - step_size * (conj_product(coil, field) + rest)
+    out_ref[1] = coil
+    out_ref[2] = dual
+
+
 def update_kernel(
-    count, lines, data_ref, table_ref, part_ref, coil_ref, base_ref, dual_ref,
-    image_ref, merged_ref, low_ref, high_ref,
+    count, lines, planes, data_ref, table_ref, parts_ref, image_ref, merged_ref, low_ref, high_ref,
+    data, table, parts, arrived,
 ):
-    planes, height, width = coil_ref.shape[1:]
-    tiles = range(pl.cdiv(planes * width, 128))
-    field = lines_back(count, lines, data_ref, table_ref, tiles) + part_ref[...]
-    for plane in range(planes):
-        normal = plane_normal(field, coil_ref, plane, plane * width)
-        for part in range(2):
-            image_new = base_ref[part, plane] - step_size * normal[part]
-            merged = image_new + dual_ref[part, plane]
-            image_ref[part, plane] = image_new
-            merged_ref[part, plane] = merged
-            if plane == 0:
-                low_ref[part] = merged
-            if plane == planes - 1:
-                high_ref[part] = merged
+    height, width = low_ref.shape[1:]
+    copies = [
+        pltpu.make_async_copy(data_ref, data, arrived.at[0]),
+        pltpu.make_async_copy(table_ref, table, arrived.at[1]),
+    ] + [pltpu.make_async_copy(parts_ref.at[i], parts.at[i], arrived.at[2 + i]) for i in range(3)]
+    for copy in copies:
+        copy.start()
+    copies[0].wait()
+    copies[1].wait()
+    field = lines_back(count, lines, data, table, range(planes * width // 128))
+    for copy in copies[2:]:
+        copy.wait()
+    image_new = parts[0] - step_size * conj_product(parts[1], field)
+    merged = image_new + parts[2]
+    image_ref[...] = image_new
+    merged_ref[...] = merged
+    for part in range(2):
+        rows = slice(part * height, (part + 1) * height)
+        low_ref[part] = merged[rows, :width]
+        high_ref[part] = merged[rows, (planes - 1) * width :]
 
 
 THRESHOLD = shrink / (half_root**3)
@@ -244,41 +288,86 @@
     lax.fori_loop(0, height // 16, body, 0, unroll=2)
 
 
-def spin_0_kernel(merged_ref, to_ref, back_ref, out_ref, bands):
-    _, planes, height, _ = merged_ref.shape
+def spins_kernel(
+    image_ref, merged_ref, to_0_ref, back_0_ref, to_1_ref, back_1_ref, half_ref, image_out, prox_out, dual_out,
+    bands, image, prox, dual, written,
+):
+    _, planes, height, width = image.shape
+
+    def cells_of(ref, plane, part):
+        return ref[part * height : (part + 1) * height, plane * width : (plane + 1) * width]
+
+    copies = [pltpu.make_async_copy(image, image_out, written.at[0])]
+    for plane in range(planes):
+        for part in range(2):
+            image[part, plane] = cells_of(image_ref, plane, part)
+    copies[0].start()
     for low in range(0, planes, 2):
         for plane in (low, low + 1):
             for part in range(2):
-                pair_lanes(merged_ref[part, plane], to_ref, bands, (plane, part))
+                pair_lanes(cells_of(merged_ref, plane, part), to_0_ref, bands, (plane, part))
         shrink_planes(0, height, bands, low, low + 1)
         for plane in (low, low + 1):
             for part in range(2):
-                out_ref[part, plane] = unpair_lanes(back_ref, bands, (plane, part), height)
-
-
-def spin_1_kernel(merged_ref, before_ref, after_ref, half_ref, to_ref, back_ref, prox_ref, dual_ref, bands):
-    _, planes, height, _ = merged_ref.shape
-
-    def cells_of(plane, part):
-        if plane < 0:
-            return before_ref[part]
-        return after_ref[part] if plane == planes else merged_ref[part, plane]
-
-    for low in range(-1, planes, 2):
+                spun = unpair_lanes(back_0_ref, bands, (plane, part), height)
+                if plane == 0:
+                    half_ref[0, part] = spun
+                elif plane == planes - 1:
+                    half_ref[1, part] = spun
+                else:
+                    prox[part, plane] = spun
+    for low in range(1, planes - 1, 2):
         for plane in (low, low + 1):
             for part in range(2):
-                pair_lanes(cells_of(plane, part), to_ref, bands, (plane + 1, part))
-        shrink_planes(1, height, bands, low + 1, low + 2)
+                pair_lanes(cells_of(merged_ref, plane, part), to_1_ref, bands, (plane, part))
+        shrink_planes(1, height, bands, low, low + 1)
         for plane in (low, low + 1):
-            if 0 <= plane < planes:
-                for part in range(2):
-                    for tile in range(2):
-                        at = (plane + 1, part, tile)
-                        bands[at + (slice(0, 1),)] = bands[at + (slice(height, height + 1),)]
-                    spun = unpair_lanes(back_ref, bands, (plane + 1, part), height)
-                    prox = half_ref[part, plane] + spun
-                    prox_ref[part, plane] = prox
-                    dual_ref[part, plane] = merged_ref[part, plane] - prox
+            for part in range(2):
+                wrap_row(bands, (plane, part), height)
+                cells = prox[part, plane] + unpair_lanes(back_1_ref, bands, (plane, part), height)
+                prox[part, plane] = cells
+                dual[part, plane] = cells_of(merged_ref, plane, part) - cells
+        own = pl.ds(low, 2)
+        for scratch, out, sem in ((prox, prox_out, low), (dual, dual_out, low + 1)):
+            copies.append(pltpu.make_async_copy(scratch.at[:, own], out.at[:, own], written.at[sem]))
+            copies[-1].start()
+    for copy in copies:
+        copy.wait()
+
+
+def wrap_row(bands, index, height):
+    for tile in range(2):
+        at = index + (tile,)
+        bands[at + (slice(0, 1),)] = bands[at + (slice(height, height + 1),)]
+
+
+def rim_kernel(
+    low_ref, high_ref, before_ref, after_ref, half_ref, to_ref, back_ref, prox_in, dual_in, prox_out, dual_out,
+    bands, prox, dual, written,
+):
+    height = low_ref.shape[1]
+    last = prox_out.shape[1] - 1
+    copies = []
+    for edge, (first, second, own) in enumerate(
+        ((before_ref, low_ref, low_ref), (high_ref, after_ref, high_ref))
+    ):
+        for plane, ref in enumerate((first, second)):
+            for part in range(2):
+                pair_lanes(ref[part], to_ref, bands, (2 * edge + plane, part))
+        shrink_planes(1, height, bands, 2 * edge, 2 * edge + 1)
+        for part in range(2):
+            index = (2 * edge + 1 - edge, part)
+            wrap_row(bands, index, height)
+            cells = half_ref[edge, part] + unpair_lanes(back_ref, bands, index, height)
+            prox[edge, part] = cells
+            dual[edge, part] = own[part] - cells
+        for scratch, out, sem in ((prox, prox_out, 2 * edge), (dual, dual_out, 2 * edge + 1)):
+            copies.append(
+                pltpu.make_async_copy(scratch.at[edge], out.at[:, edge * last], written.at[sem])
+            )
+            copies[-1].start()
+    for copy in copies:
+        copy.wait()
 
 
 def call(kernel, out_shape, micros, vmem=56, **extra):
@@ -354,18 +443,18 @@
         self.grid_len = grid_len
         _, self.planes, self.height, self.width = shape
         depth = count * self.planes
-        self.chunks = chunks = 2 if lines % 2 == 0 else 1
-        self.per_chunk = per_chunk = lines // chunks
-        self.lines = per_chunk * 2
         self.lanes = self.planes * self.width
         self.padded = pl.cdiv(self.lanes, 128) * 128
-        self.pitch = pl.cdiv(self.padded // 128 * self.lines, 8) * 8
+        first = lines // 3 * 2
+        self.chunks = [(0, first), (first, lines - first)] if first else [(0, lines)]
         freq = np.arange(grid_len)
 
         def y_order(table, axis):
-            order = np.arange(2 * grid_len).reshape(2, count, chunks, per_chunk)
-            order = order.transpose(2, 3, 0, 1).reshape(chunks, -1)
-            return [np.take(table, part, axis) for part in order]
+            order = np.arange(2 * grid_len).reshape(2, count, lines).transpose(2, 0, 1)
+            return [
+                np.take(table, order[start : start + size].reshape(-1), axis)
+                for start, size in self.chunks
+            ]
 
         forward = real_form(np.arange(self.height), freq, grid_len, -1.0).T
         self.forward_y = [three_way(part, 1) for part in y_order(forward, 0)]
@@ -379,50 +468,62 @@
             three_way(real_form(freq, np.arange(self.width), grid_len, 1.0, 1.0 / grid_len), 0),
         )
 
-
-def returned_lines(plan, image, coil_map, gain_zx):
-    count, lines = plan.count, plan.lines
-    buffer = jax.ShapeDtypeStruct((count * plan.pitch, 128), jnp.float32)
-    right = jax.ShapeDtypeStruct((6 * plan.height, plan.lanes), jnp.bfloat16)
-    first, right = call(
-        functools.partial(spread_first_kernel, count, lines), [buffer, right], 5
-    )(image, coil_map, plan.forward_y[0])
-    sent = [first]
-    for chunk in range(1, plan.chunks):
-        sent.append(
-            call(functools.partial(spread_kernel, count, lines), buffer, 3)(
-                right, plan.forward_y[chunk]
-            )
-        )
+    def buffer(self, size):
+        pitch = pl.cdiv(self.padded // 128 * size * 2, 8) * 8
+        return jax.ShapeDtypeStruct((self.count * pitch, 128), jnp.float32)
+
+
+HBM = pl.BlockSpec(memory_space=pltpu.HBM)
+VMEM = pl.BlockSpec(memory_space=pltpu.VMEM)
+
+
+def returned_lines(plan, image, coil_map, kernel):
+    count, planes, height, width = plan.count, plan.planes, plan.height, plan.width
 
     def exchange(block):
-        block = block.reshape(count, plan.pitch, 128)
-        return lax.all_to_all(block, "slab", 0, 0, tiled=True).reshape(buffer.shape)
+        parts = block.reshape(count, -1, 128)
+        return lax.all_to_all(parts, "slab", 0, 0, tiled=True).reshape(block.shape)
+
+    def spread(chunk):
+        size = plan.chunks[chunk][1]
+        table = plan.forward_y[chunk]
+        held = pltpu.VMEM((planes, 2, height, width), jnp.float32)
+        return call(
+            functools.partial(spread_kernel, count, 2 * size),
+            plan.buffer(size),
+            4,
+            in_specs=[HBM] * 3,
+            out_specs=VMEM,
+            scratch_shapes=[held, held, pltpu.VMEM(table.shape, table.dtype)]
+            + [pltpu.SemaphoreType.DMA((2 * planes + 1,))],
+        )(image, coil_map, table)
 
     whole = lambda array: pl.BlockSpec(array.shape, lambda step: (0,) * array.ndim)
+    sent = [spread(chunk) for chunk in range(len(plan.chunks))]
     returned = []
-    for chunk in range(plan.chunks):
-        data = exchange(sent[chunk])
-        at = functools.partial(lambda first, step: (first + step, 0, 0), chunk * plan.per_chunk)
+    for chunk, (start, size) in enumerate(plan.chunks):
+        buffer = plan.buffer(size)
+        group = 2 if start % 2 == 0 and size % 2 == 0 else 1
+        at = functools.partial(lambda first, step: (first + step, 0, 0), start // group)
         data = call(
-            functools.partial(middle_kernel, count, plan.planes, plan.width, lines),
+            functools.partial(middle_kernel, count, planes, width, 2 * size),
             buffer,
-            5 * plan.per_chunk,
-            grid=(plan.per_chunk,),
-            in_specs=[whole(buffer), pl.BlockSpec((1,) + gain_zx.shape[1:], at)]
+            4 * size,
+            grid=(size // group,),
+            in_specs=[whole(buffer), pl.BlockSpec((group,) + kernel.shape[1:], at)]
             + [whole(table) for table in plan.middle],
             out_specs=whole(buffer),
-        )(data, gain_zx, *plan.middle)
+        )(exchange(sent[chunk]), kernel, *plan.middle)
         returned.append(exchange(data))
     return returned
 
 
-def partial_field(plan, returned):
+def all_fields(plan, returned):
     field = jax.ShapeDtypeStruct((2 * plan.height, plan.padded), jnp.float32)
     total = ()
-    for chunk, data in enumerate(returned):
-        kernel = functools.partial(back_kernel, plan.count, plan.lines, plan.lanes)
-        total = (call(kernel, field, 4)(data, plan.back_y[chunk], *total),)
+    for (_, size), data, table in zip(plan.chunks, returned, plan.back_y):
+        kernel = functools.partial(back_kernel, plan.count, 2 * size, plan.lanes)
+        total = (call(kernel, field, 4)(data, table, *total),)
     return total[0]
 
 
@@ -433,42 +534,74 @@
     return before, after
 
 
-def finish(plan, returned, coil_map, base, dual):
+def finish(plan, returned, coil_map, image, prox_point, dual, adjoint_data):
     planes, height, width = plan.planes, plan.height, plan.width
-    part = partial_field(plan, returned[:-1])
-    plane = jax.ShapeDtypeStruct((2, height, width), jnp.float32)
-    field = jax.ShapeDtypeStruct(dual.shape, jnp.float32)
+    like = jax.ShapeDtypeStruct
+    plane = like((2, height, width), jnp.float32)
+    field = like(dual.shape, jnp.float32)
+    flat = like((2 * height, plan.lanes), jnp.float32)
+    lines = [2 * size for _, size in plan.chunks]
+    parts = like((3,) + flat.shape, jnp.float32)
+    ready = call(functools.partial(prepare_kernel, plan.count, lines[0]), parts, 9)(
+        returned[0], plan.back_y[0], image, prox_point, dual, adjoint_data, coil_map
+    )
+    data, table = returned[1], plan.back_y[1]
     image_new, merged, low, high = call(
-        functools.partial(update_kernel, plan.count, plan.lines), [field] * 2 + [plane] * 2, 8, EPI
-    )(returned[-1], plan.back_y[-1], part, coil_map, base, dual)
+        functools.partial(update_kernel, plan.count, lines[1], planes),
+        [flat] * 2 + [plane] * 2,
+        5,
+        SMALL,
+        in_specs=[HBM] * 3,
+        scratch_shapes=[
+            pltpu.VMEM(data.shape, data.dtype),
+            pltpu.VMEM(table.shape, table.dtype),
+            pltpu.VMEM(parts.shape, parts.dtype),
+            pltpu.SemaphoreType.DMA((5,)),
+        ],
+    )(data, table, ready)
     before, after = neighbours(low, high)
-    bands = lambda held: [pltpu.VMEM((held, 2, 2, height + 8, 128), jnp.float32)]
-    half = call(spin_0_kernel, field, 5, EPI, scratch_shapes=bands(planes))(
-        merged, *pairing_tables(width, 0)
-    )
-    prox, dual_new = call(spin_1_kernel, [field] * 2, 6, EPI, scratch_shapes=bands(planes + 2))(
-        merged, before, after, half, *pairing_tables(width, 1)
-    )
+    bands = lambda held: pltpu.VMEM((held, 2, 2, height + 8, 128), jnp.float32)
+    tables_0, tables_1 = pairing_tables(width, 0), pairing_tables(width, 1)
+    half, image_new, prox, dual_new = call(
+        spins_kernel,
+        [like((2,) + plane.shape, jnp.float32)] + [field] * 3,
+        6,
+        SMALL,
+        out_specs=[VMEM] + [HBM] * 3,
+        scratch_shapes=[bands(planes)]
+        + [pltpu.VMEM(field.shape, jnp.float32)] * 3
+        + [pltpu.SemaphoreType.DMA((planes,))],
+    )(image_new, merged, *tables_0, *tables_1)
+    prox, dual_new = call(
+        rim_kernel,
+        [field] * 2,
+        2,
+        SMALL,
+        in_specs=[VMEM] * 7 + [HBM] * 2,
+        out_specs=[HBM] * 2,
+        input_output_aliases={7: 0, 8: 1},
+        scratch_shapes=[bands(4)]
+        + [pltpu.VMEM((2,) + plane.shape, jnp.float32)] * 2
+        + [pltpu.SemaphoreType.DMA((4,))],
+    )(low, high, before, after, half, *tables_1, prox, dual_new)
     return image_new, prox, dual_new
 
 
 def on_device(image, prox_point, dual, adjoint_data, coil_maps, kernel):
     plan = Plan(image.shape, *kernel.shape[:2])
-    gain_zx = jnp.transpose(kernel, (0, 2, 1))
-    base = image + step_size * (adjoint_data - penalty * (image - prox_point + dual))
     coils = coil_maps.shape[0]
-    returned = [returned_lines(plan, image, coil_maps[coil], gain_zx) for coil in range(coils)]
-    alone = coils * lax.axis_size("coil") == 1
-    if alone and plan.planes % 2 == 0 and plan.height % 16 == 0 and 128 < plan.width < 256:
-        return finish(plan, returned[0], coil_maps[0], base, dual)
+    returned = [returned_lines(plan, image, coil_maps[coil], kernel) for coil in range(coils)]
+    alone = coils * lax.axis_size("coil") == 1 and len(plan.chunks) == 2
+    if alone and plan.planes % 2 == 0 and plan.lanes % 128 == 0 and plan.height % 16 == 0 and 128 < plan.width < 256:
+        return finish(plan, returned[0], coil_maps[0], image, prox_point, dual, adjoint_data)
     normal = jnp.zeros_like(image)
     for coil in range(coils):
-        field = partial_field(plan, returned[coil])
+        field = all_fields(plan, returned[coil])
         normal = normal + call(
             normal_kernel, jax.ShapeDtypeStruct(image.shape, jnp.float32), 3
         )(field, coil_maps[coil])
     normal = lax.psum(normal, "coil")
-    image_new = base - step_size * normal
+    image_new = image - step_size * (normal - adjoint_data + penalty * (image - prox_point + dual))
     merged = image_new + dual
     extended = extended_2(merged, (("slab", 1),), 1)
     first = lax.axis_index("slab") * plan.planes

time: 228 us -> 219 us (0.961)
  waiting for transfers between devices: 99.8 us -> 112 us
  local copies, waits for them, and re-layouts: 14.1 us -> 3.55 us
  other arithmetic: 5.12 us -> 0 us
  Pallas kernels: 81.8 us -> 78.2 us
    all_to_all x4, waiting for transfers between devices: 96.9 us -> 108 us  [exchange(): return lax.all_to_all(parts, 'slab', 0, 0, tiled=True).reshape(block.shape)]
    unnamed x23 -> x18, local copies, waits for them, and re-layouts: 14.1 us -> 3.55 us
    add x1 -> x0, other arithmetic: 5.12 us -> none  [on_device(): image + step_size * (adjoint_data - penalty * (image - prox_point + dual))]
    pallas_call x8, Pallas kernels: 81.8 us -> 78.2 us  [the longest x2 44 us: returned_lines(): call(functools.partial(middle_kernel, count, planes, width, 2 * size), bu...]
    ppermute x1, starting transfers between devices: 5.34 us -> 3.01 us  [neighbours(): lax.ppermute(low, 'slab', [((i + 1) % count, i) for i in range(count)])]
  transfers between devices with their start and end apart: 6 -> 6, of which waited for: 5 -> 5; matrix products, arithmetic and copies ran while one was open for 6% -> 0% of each run, Pallas kernels for 29% -> 30%
where the time goes in v2:
time: 219 us
  waiting for transfers between devices  112 us (51%)
  Pallas kernels  78.2 us (36%)
  starting transfers between devices  23.3 us (11%)
  local copies, waits for them, and re-layouts  3.55 us (2%)
    all_to_all x4, waiting for transfers between devices, exchange(): return lax.all_to_all(parts, 'slab', 0, 0, tiled=True).reshape(block.shape)  108 us
    pallas_call x2, Pallas kernels, returned_lines(): call(functools.partial(middle_kernel, count, planes, width, 2 * size), bu...  44 us
    all_to_all x4, starting transfers between devices, exchange(): return lax.all_to_all(parts, 'slab', 0, 0, tiled=True).reshape(block.shape)  20.3 us
    pallas_call x2, Pallas kernels, spread(): call(functools.partial(spread_kernel, count, 2 * size), plan.buffer(size)...  11.7 us
    pallas_call x1, Pallas kernels, finish(): call(functools.partial(prepare_kernel, plan.count, lines[0]), parts, 9)  10.7 us
    pallas_call x1, Pallas kernels, finish(): call(spins_kernel, [like((2,) + plane.shape, jnp.float32)] + [field] * 3,...  5.85 us
    ppermute x1, waiting for transfers between devices, neighbours(): lax.ppermute(high, 'slab', [(i, (i + 1) % count) for i in range(count)])  4.9 us
  transfers between devices with their start and end apart: 6, of which 5 were waited for; matrix products, arithmetic and copies ran while one was open for 0% of the time, Pallas kernels for 30%

profile of v2, /device:TPU:0, one launch (start us, length us, event | category | flops | bytes accessed | tf_op | source)
XLA Modules:
  0.0 218.5 jit_solution(17532379611053703178)
XLA Ops:
  0.6 6.9 %shard_map.195 = f32[4608,128]{1,0:T(8,128)} custom-call(f32[2,6,192,192]{3,2,1,0:T(8,128)} %image_ref.5, f32[2,6,192,192]{3,2,1,0:T(8,128)} %bitcast.17, bf16[512,1152]{1,0:T(8,128)(2,1)} %constant.24.clone.table_ref), custom_call_target="tpu_custom_call" | custom-call | flops 4000000000 | bytes 4000000 | tf_op jit(solution)/shard_map/pallas_call | solution.py:491
  7.6 7.3 %all-to-all-start.2 = ((f32[32,144,128]{2,1,0:T(8,128)}), f32[32,144,128]{2,1,0:T(8,128)S(1)}, u32[]{:S(2)}, u32[]{:S(2)}) async-start(f32[32,144,128]{2,1,0:T(8,128)} %bitcast.13), calls=%async_computation.2 | async-start | bytes 4718592 | tf_op jit(solution)/shard_map/all_to_all | solution.py:485
  14.9 4.7 %shard_map.193 = f32[2304,128]{1,0:T(8,128)} custom-call(f32[2,6,192,192]{3,2,1,0:T(8,128)} %image_ref.5, f32[2,6,192,192]{3,2,1,0:T(8,128)} %bitcast.18, bf16[256,1152]{1,0:T(8,128)(2,1)} %constant.25.clone.table_ref), custom_call_target="tpu_custom_call" | custom-call | flops 4000000000 | bytes 4000000 | tf_op jit(solution)/shard_map/pallas_call | solution.py:491
  19.6 49.8 %all-to-all-done.2 = f32[32,144,128]{2,1,0:T(8,128)S(1)} async-done(((f32[32,144,128]{2,1,0:T(8,128)}), f32[32,144,128]{2,1,0:T(8,128)S(1)}, u32[]{:S(2)}, u32[]{:S(2)}) %all-to-all-start.2) | async-done | bytes 2359328 | tf_op jit(solution)/shard_map/all_to_all | solution.py:485
  69.4 0.0 copy-start.7
  69.4 4.0 %all-to-all-start = ((f32[32,72,128]{2,1,0:T(8,128)}), f32[32,72,128]{2,1,0:T(8,128)S(1)}, u32[]{:S(2)}, u32[]{:S(2)}) async-start(f32[32,72,128]{2,1,0:T(8,128)} %bitcast.16), calls=%async_computation | async-start | bytes 2359296 | tf_op jit(solution)/shard_map/all_to_all | solution.py:485
  73.4 0.0 copy-done.7
  73.4 28.1 %shard_map.196 = f32[4608,128]{1,0:T(8,128)} custom-call(f32[4608,128]{1,0:T(8,128)} %bitcast.11, f32[12,384,384]{2,1,0:T(8,128)} %gain_ref.3, bf16[1152,768]{1,0:T(8,128)(2,1)} %constant.26.clone.fx_ref, bf16[768,1152]{1,0:T(8,128)(2,1)} %constant.27.clone.fz_ref, bf16[384,2304]{1,0:T(8,128)(2,1)} %constant.28.clone.gz_ref, ...), custom_call_target="tpu_custom_call" | custom-call | flops 32000000000 | bytes 32000000 | tf_op jit(solution)/shard_map/pallas_call | solution.py:508
  101.5 1.0 all-to-all-done
  102.5 0.0 copy-start.8
  102.5 1.0 copy-done.8
  103.5 5.1 %all-to-all-start.3 = ((f32[32,144,128]{2,1,0:T(8,128)}), f32[32,144,128]{2,1,0:T(8,128)S(1)}, u32[]{:S(2)}, u32[]{:S(2)}) async-start(f32[32,144,128]{2,1,0:T(8,128)} %bitcast.12), calls=%async_computation.3 | async-start | bytes 4718592 | tf_op jit(solution)/shard_map/all_to_all | solution.py:485
  108.6 15.9 %shard_map.194 = f32[2304,128]{1,0:T(8,128)} custom-call(f32[2304,128]{1,0:T(8,128)} %bitcast.14, f32[12,384,384]{2,1,0:T(8,128)} %gain_ref.3, bf16[1152,768]{1,0:T(8,128)(2,1)} %constant.26.clone.fx_ref, bf16[768,1152]{1,0:T(8,128)(2,1)} %constant.27.clone.fz_ref, bf16[384,2304]{1,0:T(8,128)(2,1)} %constant.28.clone.gz_ref, ...), custom_call_target="tpu_custom_call" | custom-call | flops 16000000000 | bytes 16000000 | tf_op jit(solution)/shard_map/pallas_call | solution.py:508
  124.5 38.5 %all-to-all-done.3 = f32[32,144,128]{2,1,0:T(8,128)S(1)} async-done(((f32[32,144,128]{2,1,0:T(8,128)}), f32[32,144,128]{2,1,0:T(8,128)S(1)}, u32[]{:S(2)}, u32[]{:S(2)}) %all-to-all-start.3) | async-done | bytes 2359328 | tf_op jit(solution)/shard_map/all_to_all | solution.py:485
  163.0 0.0 copy-start.6
  163.0 3.9 %all-to-all-start.1 = ((f32[32,72,128]{2,1,0:T(8,128)}), f32[32,72,128]{2,1,0:T(8,128)S(1)}, u32[]{:S(2)}, u32[]{:S(2)}) async-start(f32[32,72,128]{2,1,0:T(8,128)} %bitcast.15), calls=%async_computation.1 | async-start | bytes 2359296 | tf_op jit(solution)/shard_map/all_to_all | solution.py:485
  167.0 0.0 copy-done.6
  167.0 0.0 copy-start.2
  167.0 10.7 %shard_map.197.parts_ref = f32[3,384,1152]{2,1,0:T(8,128)} custom-call(f32[4608,128]{1,0:T(8,128)} %bitcast.10, bf16[384,1536]{1,0:T(8,128)(2,1)} %constant.30.clone.table_ref, f32[2,6,192,192]{3,2,1,0:T(8,128)} %image_ref.5, f32[2,6,192,192]{3,2,1,0:T(8,128)} %prox_ref.1, f32[2,6,192,192]{3,2,1,0:T(8,128)} %dual_ref.1, f32[2,6,192,192]{3,2,1,0:T(8,128)} %adjoint_ref.1, ...), custom_call_target="tpu_custom_call" | custom-call | flops 8999999488 | bytes 9000000 | tf_op jit(solution)/shard_map/pallas_call | solution.py:545
  177.7 18.3 %all-to-all-done.1 = f32[32,72,128]{2,1,0:T(8,128)S(1)} async-done(((f32[32,72,128]{2,1,0:T(8,128)}), f32[32,72,128]{2,1,0:T(8,128)S(1)}, u32[]{:S(2)}, u32[]{:S(2)}) %all-to-all-start.1) | async-done | bytes 1179680 | tf_op jit(solution)/shard_map/all_to_all | solution.py:485
  196.0 0.0 copy-done.2
  196.0 0.0 copy-start.5
  196.0 2.5 %copy-done.5 = f32[3,384,1152]{2,1,0:T(8,128)S(1)} copy-done((f32[3,384,1152]{2,1,0:T(8,128)S(1)}, f32[3,384,1152]{2,1,0:T(8,128)}, u32[]{:S(2)}) %copy-start.5) | copy-done | bytes 5308440
  198.5 0.0 copy-start
  198.5 0.0 copy-start.1
  198.6 0.0 copy-start.3
  198.6 0.0 copy-start.4
  198.6 3.3 %shard_map.198 = (f32[384,1152]{1,0:T(8,128)S(1)}, f32[384,1152]{1,0:T(8,128)S(1)}, f32[2,192,192]{2,1,0:T(8,128)S(1)}, f32[2,192,192]{2,1,0:T(8,128)S(1)}) custom-call(f32[2304,128]{1,0:T(8,128)S(1)} %bitcast.9, bf16[384,768]{1,0:T(8,128)(2,1)S(1)} %copy-done.2, f32[3,384,1152]{2,1,0:T(8,128)S(1)} %copy-done.5), custom_call_target="tpu_custom_call" | custom-call | flops 5000000000 | bytes 5000000 | tf_op jit(solution)/shard_map/pallas_call | solution.py:549
  201.9 3.0 %collective-permute-start.1 = (f32[2,192,192]{2,1,0:T(8,128)S(1)}, f32[2,192,192]{2,1,0:T(8,128)S(1)}, u32[]{:S(2)}, u32[]{:S(2)}) collective-permute-start(f32[2,192,192]{2,1,0:T(8,128)S(1)} %get-tuple-element.16.low_ref), channel_id=1, source_target_pairs={{1,0},{2,1},{3,2},{4,3},{5,4},{6,5},{7,6},{8,7},{9,8},{10,9},{11,1... | collective-permute-start | bytes 884744 | tf_op jit(solution)/shard_map/ppermute | solution.py:533
  204.9 0.0 collective-permute-start
  204.9 0.0 copy-done
  204.9 0.0 copy-done.1
  204.9 0.0 copy-done.3
  204.9 0.0 copy-done.4
  204.9 5.8 %shard_map.199 = (f32[2,2,192,192]{3,2,1,0:T(8,128)S(1)}, f32[2,6,192,192]{3,2,1,0:T(8,128)}, f32[2,6,192,192]{3,2,1,0:T(8,128)}, f32[2,6,192,192]{3,2,1,0:T(8,128)}) custom-call(f32[384,1152]{1,0:T(8,128)S(1)} %get-tuple-element.13.image_ref, f32[384,1152]{1,0:T(8,128)S(1)} %get-tuple-element.14.merged_ref, bf16[512,256]{1,0:T(8,128)(2,1)S(1)} %copy-done.4, ...), custom_call_target="tpu_custom_call" | custom-call | flops 6000000000 | bytes 6000000 | tf_op jit(solution)/shard_map/pallas_call | solution.py:565
  210.8 0.0 collective-permute-done.1.after_ref
  210.8 4.9 %collective-permute-done.before_ref = f32[2,192,192]{2,1,0:T(8,128)S(1)} collective-permute-done((f32[2,192,192]{2,1,0:T(8,128)S(1)}, f32[2,192,192]{2,1,0:T(8,128)S(1)}, u32[]{:S(2)}, u32[]{:S(2)}) %collective-permute-start) | collective-permute-done | bytes 294944 | tf_op jit(solution)/shard_map/ppermute | solution.py:532
  215.7 2.6 %shard_map.200 = (f32[2,6,192,192]{3,2,1,0:T(8,128)}, f32[2,6,192,192]{3,2,1,0:T(8,128)}) custom-call(f32[2,192,192]{2,1,0:T(8,128)S(1)} %get-tuple-element.16.low_ref, f32[2,192,192]{2,1,0:T(8,128)S(1)} %get-tuple-element.17.high_ref, f32[2,192,192]{2,1,0:T(8,128)S(1)} %collective-permute-done.before_ref, ...), custom_call_target="tpu_custom_call", output_to_operand_aliasing={{0}: (7, {}), {1}: (8, {})} | custom-call | flops 2000000000 | bytes 2000000 | tf_op jit(solution)/shard_map/pallas_call | solution.py:575
Async XLA Ops:
  7.6 61.8 %all-to-all-start.2 = ((f32[32,144,128]{2,1,0:T(8,128)}), f32[32,144,128]{2,1,0:T(8,128)S(1)}, u32[]{:S(2)}, u32[]{:S(2)}) async-start(f32[32,144,128]{2,1,0:T(8,128)} %bitcast.13), calls=%async_computation.2 | async-start | bytes 4718592 | tf_op jit(solution)/shard_map/all_to_all | solution.py:485
  69.4 4.0 %copy-start.7 = (f32[32,144,128]{2,1,0:T(8,128)}, f32[32,144,128]{2,1,0:T(8,128)S(1)}, u32[]{:S(2)}) copy-start(f32[32,144,128]{2,1,0:T(8,128)S(1)} %all-to-all-done.2) | copy-start | bytes 7077892
  69.4 33.1 %all-to-all-start = ((f32[32,72,128]{2,1,0:T(8,128)}), f32[32,72,128]{2,1,0:T(8,128)S(1)}, u32[]{:S(2)}, u32[]{:S(2)}) async-start(f32[32,72,128]{2,1,0:T(8,128)} %bitcast.16), calls=%async_computation | async-start | bytes 2359296 | tf_op jit(solution)/shard_map/all_to_all | solution.py:485
  102.5 1.0 copy-start.8
  103.5 59.5 %all-to-all-start.3 = ((f32[32,144,128]{2,1,0:T(8,128)}), f32[32,144,128]{2,1,0:T(8,128)S(1)}, u32[]{:S(2)}, u32[]{:S(2)}) async-start(f32[32,144,128]{2,1,0:T(8,128)} %bitcast.12), calls=%async_computation.3 | async-start | bytes 4718592 | tf_op jit(solution)/shard_map/all_to_all | solution.py:485
  163.0 4.0 %copy-start.6 = (f32[32,144,128]{2,1,0:T(8,128)}, f32[32,144,128]{2,1,0:T(8,128)S(1)}, u32[]{:S(2)}) copy-start(f32[32,144,128]{2,1,0:T(8,128)S(1)} %all-to-all-done.3) | copy-start | bytes 7077892
  163.0 33.0 %all-to-all-start.1 = ((f32[32,72,128]{2,1,0:T(8,128)}), f32[32,72,128]{2,1,0:T(8,128)S(1)}, u32[]{:S(2)}, u32[]{:S(2)}) async-start(f32[32,72,128]{2,1,0:T(8,128)} %bitcast.15), calls=%async_computation.1 | async-start | bytes 2359296 | tf_op jit(solution)/shard_map/all_to_all | solution.py:485
  167.0 29.1 %copy-start.2 = (bf16[384,768]{1,0:T(8,128)(2,1)S(1)}, bf16[384,768]{1,0:T(8,128)(2,1)}, u32[]{:S(2)}) copy-start(bf16[384,768]{1,0:T(8,128)(2,1)} %constant.31.clone.table_ref) | copy-start | bytes 1769476
  196.0 2.5 %copy-start.5 = (f32[3,384,1152]{2,1,0:T(8,128)S(1)}, f32[3,384,1152]{2,1,0:T(8,128)}, u32[]{:S(2)}) copy-start(f32[3,384,1152]{2,1,0:T(8,128)} %shard_map.197.parts_ref) | copy-start | bytes 15925252
  198.5 6.4 %copy-start = (bf16[512,192]{1,0:T(8,128)(2,1)S(1)}, bf16[512,192]{1,0:T(8,128)(2,1)}, u32[]{:S(2)}) copy-start(bf16[512,192]{1,0:T(8,128)(2,1)} %constant.35.clone.back_1_ref.back_ref) | copy-start | bytes 589828
  198.5 6.4 %copy-start.1 = (bf16[512,256]{1,0:T(8,128)(2,1)S(1)}, bf16[512,256]{1,0:T(8,128)(2,1)}, u32[]{:S(2)}) copy-start(bf16[512,256]{1,0:T(8,128)(2,1)} %constant.34.clone.to_1_ref.to_ref) | copy-start | bytes 786436
  198.6 6.4 %copy-start.3 = (bf16[512,192]{1,0:T(8,128)(2,1)S(1)}, bf16[512,192]{1,0:T(8,128)(2,1)}, u32[]{:S(2)}) copy-start(bf16[512,192]{1,0:T(8,128)(2,1)} %constant.33.clone.back_0_ref) | copy-start | bytes 589828
  198.6 6.4 %copy-start.4 = (bf16[512,256]{1,0:T(8,128)(2,1)S(1)}, bf16[512,256]{1,0:T(8,128)(2,1)}, u32[]{:S(2)}) copy-start(bf16[512,256]{1,0:T(8,128)(2,1)} %constant.32.clone.to_0_ref) | copy-start | bytes 786436
  201.9 8.9 %collective-permute-start.1 = (f32[2,192,192]{2,1,0:T(8,128)S(1)}, f32[2,192,192]{2,1,0:T(8,128)S(1)}, u32[]{:S(2)}, u32[]{:S(2)}) collective-permute-start(f32[2,192,192]{2,1,0:T(8,128)S(1)} %get-tuple-element.16.low_ref), channel_id=1, source_target_pairs={{1,0},{2,1},{3,2},{4,3},{5,4},{6,5},{7,6},{8,7},{9,8},{10,9},{11,1... | collective-permute-start | bytes 884744 | tf_op jit(solution)/shard_map/ppermute | solution.py:533
  204.9 10.8 %collective-permute-start = (f32[2,192,192]{2,1,0:T(8,128)S(1)}, f32[2,192,192]{2,1,0:T(8,128)S(1)}, u32[]{:S(2)}, u32[]{:S(2)}) collective-permute-start(f32[2,192,192]{2,1,0:T(8,128)S(1)} %get-tuple-element.17.high_ref), channel_id=1, source_target_pairs={{0,1},{1,2},{2,3},{3,4},{4,5},{5,6},{6,7},{7,8},{8,9},{9,10},{10,1... | collective-permute-start | bytes 884744 | tf_op jit(solution)/shard_map/ppermute | solution.py:532

commit v3 on v2

--- a/solution.py
+++ b/solution.py
@@ -70,28 +70,38 @@
 
 
 def spread_kernel(count, lines, image_ref, coil_ref, table_ref, out_ref, image, coil, table, arrived):
-    planes, _, _, width = image.shape
-    copies = [pltpu.make_async_copy(table_ref, table, arrived.at[2 * planes])]
-    for plane in range(planes):
-        copies.append(
-            pltpu.make_async_copy(image_ref.at[:, plane], image.at[plane], arrived.at[2 * plane])
+    _, planes, _, width = image.shape
+    groups = []
+    for low in range(0, planes, 2):
+        own = pl.ds(low, min(2, planes - low))
+        groups.append(
+            [
+                pltpu.make_async_copy(image_ref.at[:, own], image.at[:, own], arrived.at[low]),
+                pltpu.make_async_copy(coil_ref.at[:, own], coil.at[:, own], arrived.at[low + 1]),
+            ]
         )
-        copies.append(
-            pltpu.make_async_copy(coil_ref.at[:, plane], coil.at[plane], arrived.at[2 * plane + 1])
-        )
-    for copy in copies[1:3] + copies[:1] + copies[3:]:
-        copy.start()
+    groups[0].append(pltpu.make_async_copy(table_ref, table, arrived.at[2 * planes]))
+
+    def start(group):
+        for copy in groups[group]:
+            copy.start()
+
+    start(0)
     for low in range(0, planes, 2):
         reals, imags = [], []
+        if low == 0 and len(groups) > 1:
+            start(1)
+        for copy in groups[low // 2][:2]:
+            copy.wait()
+        if low // 2 + 2 < len(groups):
+            start(low // 2 + 2)
         for plane in range(low, min(low + 2, planes)):
-            copies[1 + 2 * plane].wait()
-            copies[2 + 2 * plane].wait()
-            img_r, img_i, map_r, map_i = image[plane, 0], image[plane, 1], coil[plane, 0], coil[plane, 1]
+            img_r, img_i, map_r, map_i = image[0, plane], image[1, plane], coil[0, plane], coil[1, plane]
             reals.append(map_r * img_r - map_i * img_i)
             imags.append(map_r * img_i + map_i * img_r)
         right = stacked([jnp.concatenate(reals, axis=1), jnp.concatenate(imags, axis=1)], 0)
         if low == 0:
-            copies[0].wait()
+            groups[0][2].wait()
         cells = product(table[...], right)
         for line in range(lines):
             rows = cells[line * count : (line + 1) * count]
@@ -191,11 +201,25 @@
     out_ref[2] = dual
 
 
+def close(cells):
+    half = cells.shape[0] // 2
+    tail = jnp.concatenate([cells[:half, 128:], cells[half:, 128:]], axis=1)
+    return jnp.concatenate([cells[:, :128], tail], axis=0)
+
+
+def opened(rows):
+    height = rows.shape[0] * 2 // 3
+    tail = rows[height:]
+    return jnp.concatenate(
+        [rows[:height], jnp.concatenate([tail[:, :64], tail[:, 64:]], axis=0)], axis=1
+    )
+
+
 def update_kernel(
-    count, lines, planes, data_ref, table_ref, parts_ref, image_ref, merged_ref, low_ref, high_ref,
+    count, lines, planes, data_height, data_width, data_ref, table_ref, parts_ref, image_ref, merged_ref, low_ref, high_ref,
     data, table, parts, arrived,
 ):
-    height, width = low_ref.shape[1:]
+    height, width = data_height, data_width
     copies = [
         pltpu.make_async_copy(data_ref, data, arrived.at[0]),
         pltpu.make_async_copy(table_ref, table, arrived.at[1]),
@@ -213,8 +237,8 @@
     merged_ref[...] = merged
     for part in range(2):
         rows = slice(part * height, (part + 1) * height)
-        low_ref[part] = merged[rows, :width]
-        high_ref[part] = merged[rows, (planes - 1) * width :]
+        low_ref[part] = close(merged[rows, :width])
+        high_ref[part] = close(merged[rows, (planes - 1) * width :])
 
 
 THRESHOLD = shrink / (half_root**3)
@@ -345,22 +369,22 @@
     low_ref, high_ref, before_ref, after_ref, half_ref, to_ref, back_ref, prox_in, dual_in, prox_out, dual_out,
     bands, prox, dual, written,
 ):
-    height = low_ref.shape[1]
-    last = prox_out.shape[1] - 1
+    _, planes, height, _ = prox_out.shape
+    last = planes - 1
     copies = []
     for edge, (first, second, own) in enumerate(
         ((before_ref, low_ref, low_ref), (high_ref, after_ref, high_ref))
     ):
         for plane, ref in enumerate((first, second)):
             for part in range(2):
-                pair_lanes(ref[part], to_ref, bands, (2 * edge + plane, part))
+                pair_lanes(opened(ref[part]), to_ref, bands, (2 * edge + plane, part))
         shrink_planes(1, height, bands, 2 * edge, 2 * edge + 1)
         for part in range(2):
             index = (2 * edge + 1 - edge, part)
             wrap_row(bands, index, height)
             cells = half_ref[edge, part] + unpair_lanes(back_ref, bands, index, height)
             prox[edge, part] = cells
-            dual[edge, part] = own[part] - cells
+            dual[edge, part] = opened(own[part]) - cells
         for scratch, out, sem in ((prox, prox_out, 2 * edge), (dual, dual_out, 2 * edge + 1)):
             copies.append(
                 pltpu.make_async_copy(scratch.at[edge], out.at[:, edge * last], written.at[sem])
@@ -487,7 +511,7 @@
     def spread(chunk):
         size = plan.chunks[chunk][1]
         table = plan.forward_y[chunk]
-        held = pltpu.VMEM((planes, 2, height, width), jnp.float32)
+        held = pltpu.VMEM((2, planes, height, width), jnp.float32)
         return call(
             functools.partial(spread_kernel, count, 2 * size),
             plan.buffer(size),
@@ -538,6 +562,7 @@
     planes, height, width = plan.planes, plan.height, plan.width
     like = jax.ShapeDtypeStruct
     plane = like((2, height, width), jnp.float32)
+    closed = like((2, height * 3 // 2, 128), jnp.float32)
     field = like(dual.shape, jnp.float32)
     flat = like((2 * height, plan.lanes), jnp.float32)
     lines = [2 * size for _, size in plan.chunks]
@@ -547,10 +572,10 @@
     )
     data, table = returned[1], plan.back_y[1]
     image_new, merged, low, high = call(
-        functools.partial(update_kernel, plan.count, lines[1], planes),
-        [flat] * 2 + [plane] * 2,
+        functools.partial(update_kernel, plan.count, lines[1], planes, height, width),
+        [flat] * 2 + [closed] * 2,
         5,
-        SMALL,
+        55,
         in_specs=[HBM] * 3,
         scratch_shapes=[
             pltpu.VMEM(data.shape, data.dtype),
@@ -592,7 +617,7 @@
     coils = coil_maps.shape[0]
     returned = [returned_lines(plan, image, coil_maps[coil], kernel) for coil in range(coils)]
     alone = coils * lax.axis_size("coil") == 1 and len(plan.chunks) == 2
-    if alone and plan.planes % 2 == 0 and plan.lanes % 128 == 0 and plan.height % 16 == 0 and 128 < plan.width < 256:
+    if alone and plan.planes % 2 == 0 and plan.lanes % 128 == 0 and plan.height % 16 == 0 and plan.width == 192:
         return finish(plan, returned[0], coil_maps[0], image, prox_point, dual, adjoint_data)
     normal = jnp.zeros_like(image)
     for coil in range(coils):

time: 219 us -> 217 us (level)
  waiting for transfers between devices: 112 us -> 109 us
  Pallas kernels: 78.2 us -> 80.4 us
    ppermute x1, waiting for transfers between devices: 4.9 us -> 1.1 us  [neighbours(): lax.ppermute(high, 'slab', [(i, (i + 1) % count) for i in range(count)])]
    pallas_call x1, Pallas kernels: 3.33 us -> 5.86 us  [finish(): call(functools.partial(update_kernel, plan.count, lines[1], planes, heigh...]
where the time goes in v3:
time: 217 us
  waiting for transfers between devices  109 us (50%)
  Pallas kernels  80.4 us (37%)
  starting transfers between devices  23.5 us (11%)
  local copies, waits for them, and re-layouts  2.98 us (1%)
    all_to_all x4, waiting for transfers between devices, exchange(): return lax.all_to_all(parts, 'slab', 0, 0, tiled=True).reshape(block.shape)  108 us
    pallas_call x2, Pallas kernels, returned_lines(): call(functools.partial(middle_kernel, count, planes, width, 2 * size), bu...  44.1 us
    all_to_all x4, starting transfers between devices, exchange(): return lax.all_to_all(parts, 'slab', 0, 0, tiled=True).reshape(block.shape)  20.5 us
    pallas_call x2, Pallas kernels, spread(): call(functools.partial(spread_kernel, count, 2 * size), plan.buffer(size)...  11.3 us
    pallas_call x1, Pallas kernels, finish(): call(functools.partial(prepare_kernel, plan.count, lines[0]), parts, 9)  10.7 us
    pallas_call x1, Pallas kernels, finish(): call(functools.partial(update_kernel, plan.count, lines[1], planes, heigh...  5.86 us
    pallas_call x1, Pallas kernels, finish(): call(spins_kernel, [like((2,) + plane.shape, jnp.float32)] + [field] * 3,...  5.84 us
  transfers between devices with their start and end apart: 6, of which 5 were waited for; matrix products, arithmetic and copies ran while one was open for 0% of the time, Pallas kernels for 30%

profile of v3, /device:TPU:0, one launch (start us, length us, event | category | flops | bytes accessed | tf_op | source)
XLA Modules:
  0.0 216.6 jit_solution(13833128650542863202)
XLA Ops:
  0.6 6.7 %shard_map.195 = f32[4608,128]{1,0:T(8,128)} custom-call(f32[2,6,192,192]{3,2,1,0:T(8,128)} %image_ref.5, f32[2,6,192,192]{3,2,1,0:T(8,128)} %bitcast.15, bf16[512,1152]{1,0:T(8,128)(2,1)} %constant.24.clone.table_ref), custom_call_target="tpu_custom_call" | custom-call | flops 4000000000 | bytes 4000000 | tf_op jit(solution)/shard_map/pallas_call | solution.py:515
  7.3 7.3 %all-to-all-start.2 = ((f32[32,144,128]{2,1,0:T(8,128)}), f32[32,144,128]{2,1,0:T(8,128)S(1)}, u32[]{:S(2)}, u32[]{:S(2)}) async-start(f32[32,144,128]{2,1,0:T(8,128)} %bitcast.12), calls=%async_computation.2 | async-start | bytes 4718592 | tf_op jit(solution)/shard_map/all_to_all | solution.py:509
  14.6 4.7 %shard_map.193 = f32[2304,128]{1,0:T(8,128)} custom-call(f32[2,6,192,192]{3,2,1,0:T(8,128)} %image_ref.5, f32[2,6,192,192]{3,2,1,0:T(8,128)} %bitcast.16, bf16[256,1152]{1,0:T(8,128)(2,1)} %constant.25.clone.table_ref), custom_call_target="tpu_custom_call" | custom-call | flops 4000000000 | bytes 4000000 | tf_op jit(solution)/shard_map/pallas_call | solution.py:515
  19.3 49.8 %all-to-all-done.2 = f32[32,144,128]{2,1,0:T(8,128)S(1)} async-done(((f32[32,144,128]{2,1,0:T(8,128)}), f32[32,144,128]{2,1,0:T(8,128)S(1)}, u32[]{:S(2)}, u32[]{:S(2)}) %all-to-all-start.2) | async-done | bytes 2359328 | tf_op jit(solution)/shard_map/all_to_all | solution.py:509
  69.1 0.0 copy-start.9
  69.1 4.1 %all-to-all-start = ((f32[32,72,128]{2,1,0:T(8,128)}), f32[32,72,128]{2,1,0:T(8,128)}, u32[]{:S(2)}, u32[]{:S(2)}) async-start(f32[32,72,128]{2,1,0:T(8,128)} %bitcast.14), calls=%async_computation | async-start | bytes 2359296 | tf_op jit(solution)/shard_map/all_to_all | solution.py:509
  73.3 0.0 copy-done.9
  73.3 28.1 %shard_map.196 = f32[4608,128]{1,0:T(8,128)} custom-call(f32[4608,128]{1,0:T(8,128)} %bitcast.10, f32[12,384,384]{2,1,0:T(8,128)} %gain_ref.3, bf16[1152,768]{1,0:T(8,128)(2,1)} %constant.26.clone.fx_ref, bf16[768,1152]{1,0:T(8,128)(2,1)} %constant.27.clone.fz_ref, bf16[384,2304]{1,0:T(8,128)(2,1)} %constant.28.clone.gz_ref, ...), custom_call_target="tpu_custom_call" | custom-call | flops 32000000000 | bytes 32000000 | tf_op jit(solution)/shard_map/pallas_call | solution.py:532
  101.4 0.9 all-to-all-done
  102.3 5.0 %all-to-all-start.3 = ((f32[32,144,128]{2,1,0:T(8,128)}), f32[32,144,128]{2,1,0:T(8,128)S(1)}, u32[]{:S(2)}, u32[]{:S(2)}) async-start(f32[32,144,128]{2,1,0:T(8,128)} %bitcast.11), calls=%async_computation.3 | async-start | bytes 4718592 | tf_op jit(solution)/shard_map/all_to_all | solution.py:509
  107.4 15.9 %shard_map.194 = f32[2304,128]{1,0:T(8,128)} custom-call(f32[2304,128]{1,0:T(8,128)} %bitcast.2.data_ref, f32[12,384,384]{2,1,0:T(8,128)} %gain_ref.3, bf16[1152,768]{1,0:T(8,128)(2,1)} %constant.26.clone.fx_ref, bf16[768,1152]{1,0:T(8,128)(2,1)} %constant.27.clone.fz_ref, bf16[384,2304]{1,0:T(8,128)(2,1)} %constant.28.clone.gz_ref, ...), custom_call_target="tpu_custom_call" | custom-call | flops 16000000000 | bytes 16000000 | tf_op jit(solution)/shard_map/pallas_call | solution.py:532
  123.3 38.5 %all-to-all-done.3 = f32[32,144,128]{2,1,0:T(8,128)S(1)} async-done(((f32[32,144,128]{2,1,0:T(8,128)}), f32[32,144,128]{2,1,0:T(8,128)S(1)}, u32[]{:S(2)}, u32[]{:S(2)}) %all-to-all-start.3) | async-done | bytes 2359328 | tf_op jit(solution)/shard_map/all_to_all | solution.py:509
  161.8 0.0 copy-start.8
  161.8 4.1 %all-to-all-start.1 = ((f32[32,72,128]{2,1,0:T(8,128)}), f32[32,72,128]{2,1,0:T(8,128)}, u32[]{:S(2)}, u32[]{:S(2)}) async-start(f32[32,72,128]{2,1,0:T(8,128)} %bitcast.13), calls=%async_computation.1 | async-start | bytes 2359296 | tf_op jit(solution)/shard_map/all_to_all | solution.py:509
  165.8 0.0 copy-done.8
  165.8 10.7 %shard_map.197.parts_ref = f32[3,384,1152]{2,1,0:T(8,128)} custom-call(f32[4608,128]{1,0:T(8,128)} %bitcast.9, bf16[384,1536]{1,0:T(8,128)(2,1)} %constant.30.clone.table_ref, f32[2,6,192,192]{3,2,1,0:T(8,128)} %image_ref.5, f32[2,6,192,192]{3,2,1,0:T(8,128)} %prox_ref.1, f32[2,6,192,192]{3,2,1,0:T(8,128)} %dual_ref.1, f32[2,6,192,192]{3,2,1,0:T(8,128)} %adjoint_ref.1, ...), custom_call_target="tpu_custom_call" | custom-call | flops 8999999488 | bytes 9000000 | tf_op jit(solution)/shard_map/pallas_call | solution.py:570
  176.5 18.4 %all-to-all-done.1 = f32[32,72,128]{2,1,0:T(8,128)} async-done(((f32[32,72,128]{2,1,0:T(8,128)}), f32[32,72,128]{2,1,0:T(8,128)}, u32[]{:S(2)}, u32[]{:S(2)}) %all-to-all-start.1) | async-done | bytes 1179680 | tf_op jit(solution)/shard_map/all_to_all | solution.py:509
  194.9 0.0 copy-start.2
  194.9 0.0 copy-start.3
  194.9 0.0 copy-start.4
  194.9 0.0 copy-start.5
  194.9 5.9 %shard_map.198 = (f32[384,1152]{1,0:T(8,128)}, f32[384,1152]{1,0:T(8,128)}, f32[2,288,128]{2,1,0:T(8,128)}, f32[2,288,128]{2,1,0:T(8,128)}) custom-call(f32[2304,128]{1,0:T(8,128)} %bitcast.4.data_ref, bf16[384,768]{1,0:T(8,128)(2,1)} %constant.31.clone.table_ref, f32[3,384,1152]{2,1,0:T(8,128)} %shard_map.197.parts_ref), custom_call_target="tpu_custom_call" | custom-call | flops 5000000000 | bytes 5000000 | tf_op jit(solution)/shard_map/pallas_call | solution.py:574
  200.8 3.0 %collective-permute-start.1 = (f32[2,288,128]{2,1,0:T(8,128)}, f32[2,288,128]{2,1,0:T(8,128)S(1)}, u32[]{:S(2)}, u32[]{:S(2)}) collective-permute-start(f32[2,288,128]{2,1,0:T(8,128)} %get-tuple-element.16.low_ref), channel_id=1, source_target_pairs={{1,0},{2,1},{3,2},{4,3},{5,4},{6,5},{7,6},{8,7},{9,8},{10,9},{11,1... | collective-permute-start | bytes 884744 | tf_op jit(solution)/shard_map/ppermute | solution.py:557
  203.8 0.0 collective-permute-start
  203.8 0.0 copy-done.2
  203.8 0.0 copy-done.3
  203.8 0.0 copy-done.4
  203.8 0.0 copy-done.5
  203.8 0.0 copy-start.6
  203.8 1.5 copy-done.6
  205.3 0.0 copy-start.7
  205.3 1.5 copy-done.7
  206.8 0.0 copy-start
  206.8 0.0 copy-start.1
  206.8 5.8 %shard_map.199 = (f32[2,2,192,192]{3,2,1,0:T(8,128)S(1)}, f32[2,6,192,192]{3,2,1,0:T(8,128)}, f32[2,6,192,192]{3,2,1,0:T(8,128)}, f32[2,6,192,192]{3,2,1,0:T(8,128)}) custom-call(f32[384,1152]{1,0:T(8,128)S(1)} %copy-done.6, f32[384,1152]{1,0:T(8,128)S(1)} %copy-done.7, bf16[512,256]{1,0:T(8,128)(2,1)S(1)} %copy-done.5, bf16[512,192]{1,0:T(8,128)(2,1)S(1)} %copy-done.4, ...), custom_call_target="tpu_custom_call" | custom-call | flops 6000000000 | bytes 6000000 | tf_op jit(solution)/shard_map/pallas_call | solution.py:590
  212.6 0.0 collective-permute-done.1.after_ref
  212.7 1.1 collective-permute-done.before_ref
  213.8 0.0 copy-done
  213.8 0.0 copy-done.1
  213.8 2.6 %shard_map.200 = (f32[2,6,192,192]{3,2,1,0:T(8,128)}, f32[2,6,192,192]{3,2,1,0:T(8,128)}) custom-call(f32[2,288,128]{2,1,0:T(8,128)S(1)} %copy-done, f32[2,288,128]{2,1,0:T(8,128)S(1)} %copy-done.1, f32[2,288,128]{2,1,0:T(8,128)S(1)} %collective-permute-done.before_ref, ...), custom_call_target="tpu_custom_call", output_to_operand_aliasing={{0}: (7, {}), {1}: (8, {})} | custom-call | flops 2000000000 | bytes 2000000 | tf_op jit(solution)/shard_map/pallas_call | solution.py:600
Async XLA Ops:
  7.3 61.8 %all-to-all-start.2 = ((f32[32,144,128]{2,1,0:T(8,128)}), f32[32,144,128]{2,1,0:T(8,128)S(1)}, u32[]{:S(2)}, u32[]{:S(2)}) async-start(f32[32,144,128]{2,1,0:T(8,128)} %bitcast.12), calls=%async_computation.2 | async-start | bytes 4718592 | tf_op jit(solution)/shard_map/all_to_all | solution.py:509
  69.1 4.1 %copy-start.9 = (f32[32,144,128]{2,1,0:T(8,128)}, f32[32,144,128]{2,1,0:T(8,128)S(1)}, u32[]{:S(2)}) copy-start(f32[32,144,128]{2,1,0:T(8,128)S(1)} %all-to-all-done.2) | copy-start | bytes 7077892
  69.1 33.2 %all-to-all-start = ((f32[32,72,128]{2,1,0:T(8,128)}), f32[32,72,128]{2,1,0:T(8,128)}, u32[]{:S(2)}, u32[]{:S(2)}) async-start(f32[32,72,128]{2,1,0:T(8,128)} %bitcast.14), calls=%async_computation | async-start | bytes 2359296 | tf_op jit(solution)/shard_map/all_to_all | solution.py:509
  102.3 59.4 %all-to-all-start.3 = ((f32[32,144,128]{2,1,0:T(8,128)}), f32[32,144,128]{2,1,0:T(8,128)S(1)}, u32[]{:S(2)}, u32[]{:S(2)}) async-start(f32[32,144,128]{2,1,0:T(8,128)} %bitcast.11), calls=%async_computation.3 | async-start | bytes 4718592 | tf_op jit(solution)/shard_map/all_to_all | solution.py:509
  161.8 4.1 %copy-start.8 = (f32[32,144,128]{2,1,0:T(8,128)}, f32[32,144,128]{2,1,0:T(8,128)S(1)}, u32[]{:S(2)}) copy-start(f32[32,144,128]{2,1,0:T(8,128)S(1)} %all-to-all-done.3) | copy-start | bytes 7077892
  161.8 33.1 %all-to-all-start.1 = ((f32[32,72,128]{2,1,0:T(8,128)}), f32[32,72,128]{2,1,0:T(8,128)}, u32[]{:S(2)}, u32[]{:S(2)}) async-start(f32[32,72,128]{2,1,0:T(8,128)} %bitcast.13), calls=%async_computation.1 | async-start | bytes 2359296 | tf_op jit(solution)/shard_map/all_to_all | solution.py:509
  194.9 8.9 %copy-start.2 = (bf16[512,192]{1,0:T(8,128)(2,1)S(1)}, bf16[512,192]{1,0:T(8,128)(2,1)}, u32[]{:S(2)}) copy-start(bf16[512,192]{1,0:T(8,128)(2,1)} %constant.35.clone.back_1_ref.back_ref) | copy-start | bytes 589828
  194.9 8.9 %copy-start.3 = (bf16[512,256]{1,0:T(8,128)(2,1)S(1)}, bf16[512,256]{1,0:T(8,128)(2,1)}, u32[]{:S(2)}) copy-start(bf16[512,256]{1,0:T(8,128)(2,1)} %constant.34.clone.to_1_ref.to_ref) | copy-start | bytes 786436
  194.9 8.9 %copy-start.4 = (bf16[512,192]{1,0:T(8,128)(2,1)S(1)}, bf16[512,192]{1,0:T(8,128)(2,1)}, u32[]{:S(2)}) copy-start(bf16[512,192]{1,0:T(8,128)(2,1)} %constant.33.clone.back_0_ref) | copy-start | bytes 589828
  194.9 8.9 %copy-start.5 = (bf16[512,256]{1,0:T(8,128)(2,1)S(1)}, bf16[512,256]{1,0:T(8,128)(2,1)}, u32[]{:S(2)}) copy-start(bf16[512,256]{1,0:T(8,128)(2,1)} %constant.32.clone.to_0_ref) | copy-start | bytes 786436
  200.8 11.9 %collective-permute-start.1 = (f32[2,288,128]{2,1,0:T(8,128)}, f32[2,288,128]{2,1,0:T(8,128)S(1)}, u32[]{:S(2)}, u32[]{:S(2)}) collective-permute-start(f32[2,288,128]{2,1,0:T(8,128)} %get-tuple-element.16.low_ref), channel_id=1, source_target_pairs={{1,0},{2,1},{3,2},{4,3},{5,4},{6,5},{7,6},{8,7},{9,8},{10,9},{11,1... | collective-permute-start | bytes 884744 | tf_op jit(solution)/shard_map/ppermute | solution.py:557
  203.8 10.0 %collective-permute-start = (f32[2,288,128]{2,1,0:T(8,128)}, f32[2,288,128]{2,1,0:T(8,128)S(1)}, u32[]{:S(2)}, u32[]{:S(2)}) collective-permute-start(f32[2,288,128]{2,1,0:T(8,128)} %get-tuple-element.17.high_ref), channel_id=1, source_target_pairs={{0,1},{1,2},{2,3},{3,4},{4,5},{5,6},{6,7},{7,8},{8,9},{9,10},{10,1... | collective-permute-start | bytes 884744 | tf_op jit(solution)/shard_map/ppermute | solution.py:556
  203.8 1.5 copy-start.6
  205.3 1.5 copy-start.7
  206.8 7.0 %copy-start = (f32[2,288,128]{2,1,0:T(8,128)S(1)}, f32[2,288,128]{2,1,0:T(8,128)}, u32[]{:S(2)}) copy-start(f32[2,288,128]{2,1,0:T(8,128)} %get-tuple-element.16.low_ref) | copy-start | bytes 884740
  206.8 7.0 %copy-start.1 = (f32[2,288,128]{2,1,0:T(8,128)S(1)}, f32[2,288,128]{2,1,0:T(8,128)}, u32[]{:S(2)}) copy-start(f32[2,288,128]{2,1,0:T(8,128)} %get-tuple-element.17.high_ref) | copy-start | bytes 884740
